TPU v7x, 32 devices: a whole 2x2x4 slice. The times are simulated.
32 devices in a mesh: facet: 4 (over y, x), sub: 8 (over z, core).
Axes of the slice: x: 2, y: 2, z: 4, core: 2. Of those that a mesh axis runs over, the one named last changes fastest.
Arguments:
- facet_slab: bfloat16 [4, 2, 128, 8192], P('facet', None, 'sub'), may hold values from -6 to 6
- facet_offsets: int32 [4, 2], P('facet'), may hold values from 0 to 24576
- visibility_position: float32 [2, 32768], P(None, ('facet', 'sub')), may hold values from -32 to 32
- observed: float32 [2, 32768], P(None, ('facet', 'sub')), may hold values from -3 to 3
- visibility_subgrid: int32 [32768, 1], P(('facet', 'sub')), may hold values from 0 to 63; in each aligned block of 1024 rows (0 to 1023, 1024 to 2047, ...) at most 32 rows name the same one
- clip_levels: int32 [1024], P(('facet', 'sub')), may hold values from 1 to 8
Outputs:
- facet_adjoint: float32 [4, 2, 128, 8192], P('facet', None, 'sub')
- weighted_residual: float32 [2, 32768], P(None, ('facet', 'sub'))
Inputs may be any that keep to these rules, and one draw needn't show every extreme that they name: `visibility_subgrid`: subgrid p * 8 + q covers subgrid row block p and column block q; within the rows of one device no subgrid is named more than 32 times. `facet_offsets`: column 0 is a facet's first image row, column 1 its first image column.
All inputs are finite; a program needn't handle non-finite values.
Results may differ from a plain program's by a relative error of at most 0.012.
Values may be sent and summed in bfloat16 or wider, within the bound.
A program may use at most 128 MiB of HBM per device.

v0:
```python
import math

import jax
import jax.numpy as jnp
from jax import lax
from jax.sharding import PartitionSpec as P

FS = 8192
N_IMG = 32768
SUBG = 64
PR_DEV = 2
QC_DEV = 1
VIS_BLOCK = 32


TWO_PI = 2.0 * math.pi


def phase_pair(position, frequency, image_size, factor):
    phase_index = position[:, None] * frequency[None, :] % image_size
    angles = phase_index.astype(jnp.float32) * (-TWO_PI / image_size)
    return (
        (jnp.cos(angles) * factor).astype(jnp.bfloat16),
        (jnp.sin(angles) * factor).astype(jnp.bfloat16),
    )


def column_tables(col_offset, facet_width, image_size, subgrid_size, column_count):
    position = col_offset + jnp.arange(facet_width, dtype=jnp.int32)
    fine_cos, fine_sin = phase_pair(
        position, jnp.arange(subgrid_size, dtype=jnp.int32), image_size, facet_width ** (-0.5)
    )
    coarse_freq = jnp.arange(column_count, dtype=jnp.int32) * (image_size // column_count)
    coarse_cos, coarse_sin = phase_pair(position, coarse_freq, image_size, 1.0)
    return (fine_cos, fine_sin, coarse_cos, coarse_sin)


def row_tables(position, image_size, subgrid_size, row_blocks, total_rows):
    block_start = jnp.arange(row_blocks, dtype=jnp.int32)[:, None] * (image_size // row_blocks)
    frequency = (block_start + jnp.arange(subgrid_size, dtype=jnp.int32)[None, :]).reshape(-1)
    return phase_pair(position, frequency, image_size, 0.5 * total_rows ** (-0.5))


def column_forward(slab_real, slab_imag, tables):
    fine_cos, fine_sin, coarse_cos, coarse_sin = tables
    facet_width = fine_cos.shape[0]
    column_count = coarse_cos.shape[1]
    row_count = slab_real.shape[0]
    grouping = 4
    forward_matrix = jnp.concatenate(
        [jnp.concatenate([fine_cos, fine_sin], 1), jnp.concatenate([-fine_sin, fine_cos], 1)], 0
    )
    real_wide = slab_real.astype(jnp.float32)[None]
    imag_wide = slab_imag.astype(jnp.float32)[None]

    def one_group(cos_sin):
        cos_group = cos_sin[0].astype(jnp.float32)[:, None, :]
        sin_group = cos_sin[1].astype(jnp.float32)[:, None, :]
        mod_real = (real_wide * cos_group - imag_wide * sin_group).astype(jnp.bfloat16)
        mod_imag = (real_wide * sin_group + imag_wide * cos_group).astype(jnp.bfloat16)
        joined = jnp.concatenate([mod_real, mod_imag], 2).reshape(
            grouping * row_count, 2 * facet_width
        )
        return jnp.dot(joined, forward_matrix, preferred_element_type=jnp.float32).reshape(
            grouping, row_count, -1
        )

    cos_groups = coarse_cos.T.reshape(column_count // grouping, grouping, facet_width)
    sin_groups = coarse_sin.T.reshape(column_count // grouping, grouping, facet_width)
    spectra = lax.map(one_group, (cos_groups, sin_groups))
    spectra = spectra.reshape(column_count, row_count, -1).transpose(1, 0, 2)
    return spectra.astype(jnp.bfloat16)


def row_forward(row_cos, row_sin, spectra):
    half_width = spectra.shape[2] // 2
    swapped = jnp.concatenate([-spectra[:, :, half_width:], spectra[:, :, :half_width]], 2)
    stacked = jnp.concatenate([spectra, swapped], 0)
    left_rows = jnp.concatenate([row_cos, row_sin], 0)
    flat = stacked.reshape(stacked.shape[0], -1)
    result = jnp.dot(left_rows.T, flat, preferred_element_type=jnp.float32)
    return result.reshape(left_rows.shape[1], spectra.shape[1], spectra.shape[2])


def row_adjoint(row_cos, row_sin, corrected_rows):
    half_width = corrected_rows.shape[2] // 2
    swapped = jnp.concatenate(
        [corrected_rows[:, :, half_width:], -corrected_rows[:, :, :half_width]], 2
    )
    stacked = jnp.concatenate([corrected_rows, swapped], 0)
    left_rows = jnp.concatenate([row_cos, row_sin], 1)
    flat = stacked.reshape(stacked.shape[0], -1)
    result = jnp.dot(left_rows, flat, preferred_element_type=jnp.float32)
    return result.reshape(left_rows.shape[0], corrected_rows.shape[1], corrected_rows.shape[2])


def column_adjoint(images, tables):
    fine_cos, fine_sin, coarse_cos, coarse_sin = tables
    facet_width = fine_cos.shape[0]
    row_count = images.shape[0]
    column_count = images.shape[1]
    grouping = 4
    adjoint_matrix = jnp.concatenate(
        [
            jnp.concatenate([fine_cos.T, -fine_sin.T], 1),
            jnp.concatenate([fine_sin.T, fine_cos.T], 1),
        ],
        0,
    )
    image_groups = images.transpose(1, 0, 2).reshape(
        column_count // grouping, grouping * row_count, images.shape[2]
    )
    cos_groups = coarse_cos.T.reshape(column_count // grouping, grouping, facet_width)
    sin_groups = coarse_sin.T.reshape(column_count // grouping, grouping, facet_width)

    def accumulate(running, inputs):
        image_group, cos_group, sin_group = inputs
        spread = jnp.dot(image_group, adjoint_matrix, preferred_element_type=jnp.float32).reshape(
            grouping, row_count, 2 * facet_width
        )
        spread_real = spread[:, :, :facet_width]
        spread_imag = spread[:, :, facet_width:]
        cos_wide = cos_group.astype(jnp.float32)[:, None, :]
        sin_wide = sin_group.astype(jnp.float32)[:, None, :]
        new_real = running[0] + jnp.sum(cos_wide * spread_real + sin_wide * spread_imag, 0)
        new_imag = running[1] + jnp.sum(cos_wide * spread_imag - sin_wide * spread_real, 0)
        return ((new_real, new_imag), None)

    initial = (
        jnp.zeros((row_count, facet_width), jnp.float32),
        jnp.zeros((row_count, facet_width), jnp.float32),
    )
    finals, unused = lax.scan(accumulate, initial, (image_groups, cos_groups, sin_groups))
    return jnp.stack([finals[0], finals[1]])


def subgrid_pass(subgrids, payload, live_mask):
    subgrid_size = subgrids.shape[1]
    local_count = subgrids.shape[0]
    factor = subgrid_size ** (-0.5)
    offsets_grid = jnp.arange(subgrid_size, dtype=jnp.float32) * (TWO_PI / subgrid_size)
    angle_left = payload[0][:, :, None] * offsets_grid
    angle_right = payload[1][:, :, None] * offsets_grid
    left_real = jnp.cos(angle_left) * factor
    left_imag = jnp.sin(angle_left) * factor
    right_real = (jnp.cos(angle_right) * factor).astype(jnp.bfloat16)
    right_imag = (jnp.sin(angle_right) * factor).astype(jnp.bfloat16)
    first_basis = jnp.concatenate([right_real, -right_imag], 2)
    second_basis = jnp.concatenate([right_imag, right_real], 2)
    inner_real = jnp.stack(
        [
            jnp.dot(first_basis[item], subgrids[item].T, preferred_element_type=jnp.float32)
            for item in range(local_count)
        ]
    )
    inner_imag = jnp.stack(
        [
            jnp.dot(second_basis[item], subgrids[item].T, preferred_element_type=jnp.float32)
            for item in range(local_count)
        ]
    )
    predicted_real = jnp.sum(left_real * inner_real - left_imag * inner_imag, 2)
    predicted_imag = jnp.sum(left_real * inner_imag + left_imag * inner_real, 2)
    misfit_real = payload[2] - predicted_real
    misfit_imag = payload[3] - predicted_imag
    threshold = payload[4] + (1.0 - live_mask)
    magnitude = jnp.sqrt(misfit_real * misfit_real + misfit_imag * misfit_imag)
    weight = live_mask * threshold / jnp.maximum(magnitude, threshold)
    weighted_real = weight * misfit_real
    weighted_imag = weight * misfit_imag
    phasor_real = (
        left_real * weighted_real[:, :, None] + left_imag * weighted_imag[:, :, None]
    ).astype(jnp.bfloat16)
    phasor_imag = (
        left_real * weighted_imag[:, :, None] - left_imag * weighted_real[:, :, None]
    ).astype(jnp.bfloat16)
    phasors = jnp.concatenate([phasor_real, phasor_imag], 1)
    bases = jnp.concatenate([first_basis, second_basis], 1)
    gridded = jnp.stack(
        [
            jnp.dot(phasors[item].T, bases[item], preferred_element_type=jnp.float32)
            for item in range(local_count)
        ]
    )
    return (gridded.astype(jnp.bfloat16), weighted_real, weighted_imag)


def on_device(
    facet_slab, facet_offsets, visibility_position, observed, visibility_subgrid, clip_levels
):
    sub_count = lax.axis_size("sub")
    facet_count = lax.axis_size("facet")
    devices = sub_count * facet_count
    rows_dev = facet_slab.shape[2]
    total_rows = rows_dev * sub_count
    column_count = QC_DEV * sub_count
    row_blocks = PR_DEV * facet_count
    local_count = PR_DEV * QC_DEV
    vis_count = visibility_position.shape[1]
    most_slots = max(2, 2 * vis_count // (row_blocks * column_count))
    row_offset = facet_offsets[0, 0]
    tables = column_tables(facet_offsets[0, 1], FS, N_IMG, SUBG, column_count)
    spectra = column_forward(facet_slab[0, 0], facet_slab[0, 1], tables)
    own_rows = row_offset + lax.axis_index("sub") * rows_dev + jnp.arange(rows_dev, dtype=jnp.int32)
    row_cos, row_sin = row_tables(own_rows, N_IMG, SUBG, row_blocks, total_rows)
    partial_sum = row_forward(row_cos, row_sin, spectra)
    arranged = partial_sum.reshape(facet_count, PR_DEV, SUBG, sub_count, QC_DEV, 2 * SUBG)
    arranged = arranged.transpose(0, 3, 1, 4, 2, 5).reshape(devices * local_count, SUBG, 2 * SUBG)
    summed = lax.psum_scatter(arranged, ("facet", "sub"), scatter_dimension=0, tiled=True)
    subgrids = summed.astype(jnp.bfloat16)
    identity = visibility_subgrid[:, 0]
    block_row = identity // column_count
    block_col = identity % column_count
    owner = block_row // PR_DEV * sub_count + block_col // QC_DEV
    local_index = block_row % PR_DEV * QC_DEV + block_col % QC_DEV
    sort_order = jnp.argsort(identity, stable=True)
    sorted_ids = identity[sort_order]
    first_seen = jnp.searchsorted(sorted_ids, sorted_ids, side="left")
    ranked_sorted = jnp.arange(vis_count, dtype=jnp.int32) - first_seen
    ranked = jnp.zeros((vis_count,), jnp.int32).at[sort_order].set(ranked_sorted)
    slot_index = (owner * local_count + local_index) * most_slots + ranked
    slot_total = devices * local_count * most_slots
    levels = jnp.repeat(clip_levels, VIS_BLOCK).astype(jnp.float32) * 0.25
    rows_send = jnp.stack(
        [visibility_position[0], visibility_position[1], observed[0], observed[1], levels]
    )
    payload_out = jnp.zeros((5, slot_total), jnp.float32).at[:, slot_index].set(rows_send)
    live_out = jnp.zeros((1, slot_total), jnp.float32).at[0, slot_index].set(1.0)
    payload_in, live_in = (
        lax.all_to_all(
            payload_out.reshape(5, devices, -1),
            ("facet", "sub"),
            split_axis=1,
            concat_axis=1,
            tiled=True,
        ),
        lax.all_to_all(
            live_out.reshape(1, devices, -1),
            ("facet", "sub"),
            split_axis=1,
            concat_axis=1,
            tiled=True,
        ),
    )
    payload = (
        payload_in.reshape(5, devices, local_count, most_slots)
        .transpose(0, 2, 1, 3)
        .reshape(5, local_count, devices * most_slots)
    )
    live_mask = (
        live_in.reshape(devices, local_count, most_slots)
        .transpose(1, 0, 2)
        .reshape(local_count, devices * most_slots)
    )
    corrected, weighted_real, weighted_imag = subgrid_pass(subgrids, payload, live_mask)
    weighted_back = jnp.stack([weighted_real, weighted_imag]).reshape(
        2, local_count, devices, most_slots
    )
    weighted_back = weighted_back.transpose(0, 2, 1, 3).reshape(
        2, devices, local_count * most_slots
    )
    returned = lax.all_to_all(
        weighted_back, ("facet", "sub"), split_axis=1, concat_axis=1, tiled=True
    )
    weighted_residual = returned.reshape(2, slot_total)[:, slot_index]
    everything = lax.all_gather(corrected, ("facet", "sub"), axis=0, tiled=True)
    ordered = everything.reshape(facet_count, sub_count, PR_DEV, QC_DEV, SUBG, 2 * SUBG)
    ordered = ordered.transpose(0, 2, 4, 1, 3, 5).reshape(row_blocks * SUBG, column_count, 2 * SUBG)
    images = row_adjoint(row_cos, row_sin, ordered).astype(jnp.bfloat16)
    facet_adjoint = column_adjoint(images, tables)[None]
    return (facet_adjoint, weighted_residual)


def solution(mesh):
    placed = (
        P("facet", None, "sub", None),
        P("facet", None),
        P(None, ("facet", "sub")),
        P(None, ("facet", "sub")),
        P(("facet", "sub"), None),
        P(("facet", "sub")),
    )
    return jax.shard_map(
        on_device,
        mesh=mesh,
        in_specs=placed,
        out_specs=(P("facet", None, "sub", None), P(None, ("facet", "sub"))),
        check_vma=False,
    )
```

profile of v0, /device:TPU:0, one launch (start us, length us, event | category | flops | bytes accessed | tf_op | source)
XLA Modules:
  0.0 299.0 jit_solution(5154226547301820697)
XLA Ops:
  7.2 1.3 fusion.110
  8.5 0.6 iota_add_fusion
  9.2 20.3 %multiply_convert_fusion = (bf16[8192,64]{1,0:T(8,128)(2,1)S(1)}, bf16[8192,64]{1,0:T(8,128)(2,1)}) fusion(s32[8192]{0:T(1024)S(1)} %iota_add_fusion), kind=kLoop, calls=%fused_computation.39 | loop fusion | flops 9437184 | bytes 2129920 | tf_op jit(solution)/shard_map/convert_element_type | solution.py:24
  29.5 18.9 %fusion.37 = bf16[8192,64]{1,0:T(8,128)(2,1)} fusion(s32[8192]{0:T(1024)S(1)} %iota_add_fusion), kind=kLoop, calls=%fused_computation.86 | loop fusion | flops 9961472 | bytes 1081344 | tf_op jit(solution)/shard_map/neg | solution.py:51
  48.4 2.3 sine_convert_fusion
  50.6 1.1 bitcast_convert_fusion.4
  51.8 12.2 %maximum_maximum_fusion = bf16[16384,128]{1,0:T(8,128)(2,1)} fusion(bf16[8192,64]{1,0:T(8,128)(2,1)} %get-tuple-element.274, bf16[8192,64]{1,0:T(8,128)(2,1)} %fusion.37, bf16[8192,64]{1,0:T(8,128)(2,1)S(1)} %get-tuple-element.273), kind=kLoop, calls=%fused_computation.37 | loop fusion | flops 16777216 | bytes 7340032 | tf_op jit(solution)/shard_map/concatenate | solution.py:50
  64.0 7.3 %while.48 = (s32[]{:T(128)}, bf16[2,4,16,128]{3,2,1,0:T(8,128)(2,1)S(1)}, f32[1,16,8192]{2,1,0:T(8,128)S(1)}, bf16[2,4,8192]{2,1,0:T(4,128)(2,1)S(1)}, f32[1,16,...) while((s32[]{:T(128)}, ...), condition=%wide.region_7.8_spmd, body=%wide.region_6.7_spmd.sunk | while | flops 276889600 | bytes 10125405 | solution.py:70
  64.5 3.1 %fusion.119 = bf16[2,4,16,128]{3,2,1,0:T(8,128)(2,1)S(1)} fusion(bf16[2,4,16,128]{3,2,1,0:T(8,128)(2,1)S(1)} %get-tuple-element.448, s32[]{:T(128)} %get-tuple-element.447, bf16[16384,128]{1,0:T(8,128)(2,1)} %get-tuple-element.461, bf16[1,4,16,8192]{3,2,1,0:T(8,128)(2,1)S(1)} %get-tuple-element.399, bf16[1,4,16,8192]{3,2,1,0:T(8,128)(2,1)S(1)} %get-tuple-element.400), kind=kOutput, calls=%fused_computation.14.clone.1 | convolution fusion | flops 272629760 | bytes 6324228 | tf_op jit(solution)/shard_map/while/body/eval_jaxpr/dot_general | solution.py:64
  68.2 3.1 %fusion.119 = bf16[2,4,16,128]{3,2,1,0:T(8,128)(2,1)S(1)} fusion(bf16[2,4,16,128]{3,2,1,0:T(8,128)(2,1)S(1)} %get-tuple-element.448, s32[]{:T(128)} %get-tuple-element.447, bf16[16384,128]{1,0:T(8,128)(2,1)} %get-tuple-element.461, bf16[1,4,16,8192]{3,2,1,0:T(8,128)(2,1)S(1)} %get-tuple-element.399, bf16[1,4,16,8192]{3,2,1,0:T(8,128)(2,1)S(1)} %get-tuple-element.400), kind=kOutput, calls=%fused_computation.14.clone.1 | convolution fusion | flops 272629760 | bytes 6324228 | tf_op jit(solution)/shard_map/while/body/eval_jaxpr/dot_general | solution.py:64
  73.1 1.5 copy.100
  74.6 0.6 copy-done
  75.3 4.4 %sort.17 = (s32[1024]{0:T(1024)}, s32[1024]{0:T(1024)S(1)}) sort(s32[1024]{0:T(1024)S(1)} %bitcast.212, s32[1024]{0:T(1024)S(1)} %iota.60), dimensions={0}, to_apply=%region_0.1 | sort | flops 10240 | bytes 16384 | tf_op jit(solution)/shard_map/jit(argsort)/sort | solution.py:216
  79.6 4.5 %gather_fusion.1 = s32[1024]{0:T(1024)S(1)} fusion(s32[1024]{0:T(1024)S(1)} %bitcast.213, s32[1024]{0:T(1024)S(1)} %get-tuple-element.279), kind=kCustom, calls=%fused_computation.1 | custom fusion | bytes 12288 | tf_op jit(solution)/shard_map/gather | solution.py:217
  84.2 50.7 %while.49 = (s32[]{:T(128)}, u32[1024]{0:T(1024)S(1)}, u32[1024]{0:T(1024)S(1)}, s32[1024]{0:T(1024)S(1)}, s32[]{:T(128)}, /*index=5*/s32[]{:T(128)}, s32[]{}) while((s32[]{:T(128)}, u32[1024]{0:T(1024)S(1)}, u32[1024]{0:T(1024)S(1)}, s32[1024]{0:T(1024)S(1)}, s32[]{:T(128)}, /*index=5*/s32[]{:T(128)}, s32[]{}) %tuple.109), condition=%wide.region_2.3_spmd.clone, body=%wide.region_1.2_spmd.clone.sunk | while | flops 19460 | bytes 67685 | solution.py:218
  84.2 4.5 %gather_fusion = s32[1024]{0:T(1024)S(1)} fusion(s32[1024]{0:T(1024)S(1)} %get-tuple-element.435, u32[1024]{0:T(1024)S(1)} %broadcast_clamp_fusion.4), kind=kCustom, calls=%fused_computation.clone.clone.1 | custom fusion | bytes 12288 | tf_op jit(solution)/shard_map/jit(searchsorted)/jit(_searchsorted_scan_impl)/vmap(jit(_searchsorted_scan_impl))/while/body/eval_jaxpr/gather | solution.py:218
  88.8 4.5 %gather_fusion = s32[1024]{0:T(1024)S(1)} fusion(s32[1024]{0:T(1024)S(1)} %get-tuple-element.435, u32[1024]{0:T(1024)S(1)} %broadcast_clamp_fusion.4), kind=kCustom, calls=%fused_computation.clone.clone.1 | custom fusion | bytes 12288 | tf_op jit(solution)/shard_map/jit(searchsorted)/jit(_searchsorted_scan_impl)/vmap(jit(_searchsorted_scan_impl))/while/body/eval_jaxpr/gather | solution.py:218
  93.5 4.5 %gather_fusion = s32[1024]{0:T(1024)S(1)} fusion(s32[1024]{0:T(1024)S(1)} %get-tuple-element.435, u32[1024]{0:T(1024)S(1)} %broadcast_clamp_fusion.4), kind=kCustom, calls=%fused_computation.clone.clone.1 | custom fusion | bytes 12288 | tf_op jit(solution)/shard_map/jit(searchsorted)/jit(_searchsorted_scan_impl)/vmap(jit(_searchsorted_scan_impl))/while/body/eval_jaxpr/gather | solution.py:218
  98.1 4.5 %gather_fusion = s32[1024]{0:T(1024)S(1)} fusion(s32[1024]{0:T(1024)S(1)} %get-tuple-element.435, u32[1024]{0:T(1024)S(1)} %broadcast_clamp_fusion.4), kind=kCustom, calls=%fused_computation.clone.clone.1 | custom fusion | bytes 12288 | tf_op jit(solution)/shard_map/jit(searchsorted)/jit(_searchsorted_scan_impl)/vmap(jit(_searchsorted_scan_impl))/while/body/eval_jaxpr/gather | solution.py:218
  102.7 4.5 %gather_fusion = s32[1024]{0:T(1024)S(1)} fusion(s32[1024]{0:T(1024)S(1)} %get-tuple-element.435, u32[1024]{0:T(1024)S(1)} %broadcast_clamp_fusion.4), kind=kCustom, calls=%fused_computation.clone.clone.1 | custom fusion | bytes 12288 | tf_op jit(solution)/shard_map/jit(searchsorted)/jit(_searchsorted_scan_impl)/vmap(jit(_searchsorted_scan_impl))/while/body/eval_jaxpr/gather | solution.py:218
  107.3 4.5 %gather_fusion = s32[1024]{0:T(1024)S(1)} fusion(s32[1024]{0:T(1024)S(1)} %get-tuple-element.435, u32[1024]{0:T(1024)S(1)} %broadcast_clamp_fusion.4), kind=kCustom, calls=%fused_computation.clone.clone.1 | custom fusion | bytes 12288 | tf_op jit(solution)/shard_map/jit(searchsorted)/jit(_searchsorted_scan_impl)/vmap(jit(_searchsorted_scan_impl))/while/body/eval_jaxpr/gather | solution.py:218
  111.9 4.5 %gather_fusion = s32[1024]{0:T(1024)S(1)} fusion(s32[1024]{0:T(1024)S(1)} %get-tuple-element.435, u32[1024]{0:T(1024)S(1)} %broadcast_clamp_fusion.4), kind=kCustom, calls=%fused_computation.clone.clone.1 | custom fusion | bytes 12288 | tf_op jit(solution)/shard_map/jit(searchsorted)/jit(_searchsorted_scan_impl)/vmap(jit(_searchsorted_scan_impl))/while/body/eval_jaxpr/gather | solution.py:218
  116.5 4.5 %gather_fusion = s32[1024]{0:T(1024)S(1)} fusion(s32[1024]{0:T(1024)S(1)} %get-tuple-element.435, u32[1024]{0:T(1024)S(1)} %broadcast_clamp_fusion.4), kind=kCustom, calls=%fused_computation.clone.clone.1 | custom fusion | bytes 12288 | tf_op jit(solution)/shard_map/jit(searchsorted)/jit(_searchsorted_scan_impl)/vmap(jit(_searchsorted_scan_impl))/while/body/eval_jaxpr/gather | solution.py:218
  121.1 4.5 %gather_fusion = s32[1024]{0:T(1024)S(1)} fusion(s32[1024]{0:T(1024)S(1)} %get-tuple-element.435, u32[1024]{0:T(1024)S(1)} %broadcast_clamp_fusion.4), kind=kCustom, calls=%fused_computation.clone.clone.1 | custom fusion | bytes 12288 | tf_op jit(solution)/shard_map/jit(searchsorted)/jit(_searchsorted_scan_impl)/vmap(jit(_searchsorted_scan_impl))/while/body/eval_jaxpr/gather | solution.py:218
  125.7 4.5 %gather_fusion = s32[1024]{0:T(1024)S(1)} fusion(s32[1024]{0:T(1024)S(1)} %get-tuple-element.435, u32[1024]{0:T(1024)S(1)} %broadcast_clamp_fusion.4), kind=kCustom, calls=%fused_computation.clone.clone.1 | custom fusion | bytes 12288 | tf_op jit(solution)/shard_map/jit(searchsorted)/jit(_searchsorted_scan_impl)/vmap(jit(_searchsorted_scan_impl))/while/body/eval_jaxpr/gather | solution.py:218
  130.4 4.5 %gather_fusion = s32[1024]{0:T(1024)S(1)} fusion(s32[1024]{0:T(1024)S(1)} %get-tuple-element.435, u32[1024]{0:T(1024)S(1)} %broadcast_clamp_fusion.4), kind=kCustom, calls=%fused_computation.clone.clone.1 | custom fusion | bytes 12288 | tf_op jit(solution)/shard_map/jit(searchsorted)/jit(_searchsorted_scan_impl)/vmap(jit(_searchsorted_scan_impl))/while/body/eval_jaxpr/gather | solution.py:218
  135.0 4.5 %scatter_custom_fusion = s32[1024]{0:T(1024)S(1)} fusion(s32[1024]{0:T(1024)S(1)} %get-tuple-element.280, s32[1024]{0:T(1024)S(1)} %convert_subtract_fusion, s32[]{:T(128)} %constant.168.clone.1), kind=kCustom, calls=%fused_computation.212 | custom fusion | bytes 4100 | tf_op jit(solution)/shard_map/scatter | solution.py:220
  139.7 4.3 %scatter_custom_fusion.2 = f32[2048]{0:T(1024)S(1)} fusion(s32[1024]{0:T(1024)S(1)} %broadcast_select_fusion, f32[1024]{0:T(1024)S(1)} %broadcast.280, f32[]{:T(128)} %constant.169.clone.1), kind=kCustom, calls=%fused_computation.197 | custom fusion | bytes 8196
  144.1 0.7 reshape.331
  144.7 7.3 %all-to-all-start.1 = ((f32[1,32,64]{2,0,1:T(1,128)}), f32[1,32,64]{2,0,1:T(1,128)S(1)}, u32[]{:S(2)}, u32[]{:S(2)}) async-start(f32[1,32,64]{2,0,1:T(1,128)} %reshape.331), calls=%async_computation.1 | async-start | bytes 32768 | tf_op jit(solution)/shard_map/all_to_all | solution.py:237
  152.2 8.6 %multiply_convert_fusion.2 = (bf16[64,8192]{1,0:T(8,128)(2,1)S(1)}, bf16[64,8192]{1,0:T(8,128)(2,1)S(1)}) fusion(s32[8192]{0:T(1024)S(1)} %iota_add_fusion), kind=kLoop, calls=%fused_computation.51 | loop fusion | flops 9437184 | bytes 2129920 | tf_op jit(solution)/shard_map/convert_element_type | solution.py:24
  161.1 4.1 %scatter_custom_fusion.1 = f32[5,2048]{0,1:T(8,128)} fusion(s32[1024]{0:T(1024)S(1)} %get-tuple-element.246, f32[1024,5]{1,0:T(8,128)S(1)} %copy.92, f32[]{:T(128)} %constant.169.clone.1), kind=kCustom, calls=%fused_computation.109 | custom fusion | bytes 40964 | tf_op jit(solution)/shard_map/scatter | solution.py:227
  165.1 1.6 copy.93
  166.7 0.7 reshape.432
  167.5 5.8 %all-to-all-start = ((f32[32,1,320]{2,1,0:T(1,128)}), f32[32,1,320]{2,1,0:T(1,128)S(1)}, u32[]{:S(2)}, u32[]{:S(2)}) async-start(f32[32,1,320]{2,1,0:T(1,128)} %reshape.432), calls=%async_computation | async-start | bytes 98304 | tf_op jit(solution)/shard_map/all_to_all | solution.py:230
  173.9 0.7 reduce.7
  174.8 6.1 %all-to-all-done = f32[32,1,320]{2,1,0:T(1,128)S(1)} async-done(((f32[32,1,320]{2,1,0:T(1,128)}), f32[32,1,320]{2,1,0:T(1,128)S(1)}, u32[]{:S(2)}, u32[]{:S(2)}) %all-to-all-start) | async-done | bytes 40992 | tf_op jit(solution)/shard_map/all_to_all | solution.py:230
  181.3 0.8 reduce.8
  182.5 1.9 fusion.76
  184.5 2.2 fusion.49
  186.7 1.1 maximum_maximum_fusion.2
  187.7 27.0 %reduce-scatter.2.cloned.1.call-done = f32[2,64,128]{2,1,0:T(8,128)} async-done(((f32[64,64,128]{2,1,0:T(8,128)}), f32[2,64,128]{2,1,0:T(8,128)}) %reduce-scatter.2.cloned.1.call-update) | async-done | bytes 65552 | tf_op jit(solution)/shard_map/reduce_scatter | solution.py:209
  214.8 0.8 convert_element_type.208
  216.3 2.5 fusion.39
  219.4 2.1 fusion.43
  221.5 1.4 fusion.25
  222.9 1.3 fusion.26
  224.2 0.6 pad_maximum_fusion.6
  224.9 8.6 %fusion.73 = bf16[64,8192]{1,0:T(8,128)(2,1)} fusion(s32[8192]{0:T(1024)S(1)} %iota_add_fusion), kind=kLoop, calls=%fused_computation.138 | loop fusion | flops 9961472 | bytes 1081344 | tf_op jit(solution)/shard_map/neg | solution.py:105
  233.6 0.7 reshape.434
  234.3 2.7 all-to-all-start.2
  237.0 12.5 %maximum_maximum_fusion.1 = bf16[128,16384]{1,0:T(8,128)(2,1)} fusion(bf16[64,8192]{1,0:T(8,128)(2,1)S(1)} %get-tuple-element.270, bf16[64,8192]{1,0:T(8,128)(2,1)S(1)} %get-tuple-element.269, bf16[64,8192]{1,0:T(8,128)(2,1)} %fusion.73), kind=kLoop, calls=%fused_computation.38 | loop fusion | flops 16777216 | bytes 7340032 | tf_op jit(solution)/shard_map/concatenate | solution.py:103
  249.6 0.7 reduce.9
  250.8 2.8 gather_fusion.2
  253.6 0.8 copy.107
  254.4 20.6 %all-gather.2.cloned.1.call-done = bf16[64,64,128]{2,1,0:T(8,128)(2,1)} async-done(((bf16[2,64,128]{2,1,0:T(8,128)(2,1)}), bf16[64,64,128]{2,1,0:T(8,128)(2,1)}) %all-gather.2.cloned.1.call-update) | async-done | bytes 1048592 | tf_op jit(solution)/shard_map/all_gather | solution.py:266
  275.0 1.9 copy.101
  278.4 1.5 maximum_bitcast_fusion.6
  279.9 2.9 copy.103
  282.7 0.6 convolution_convert_fusion
  283.4 7.7 %while.50 = (s32[]{:T(128)}, f32[16,8192]{1,0:T(8,128)S(1)}, f32[16,8192]{1,0:T(8,128)S(1)}, bf16[2,4,8192]{2,1,0:T(4,128)(2,1)S(1)}, bf16[2,64,128]{2,1,0:T(8,1...) while((s32[]{:T(128)}, f32[16,8192]{1,0:T(8,128)S(1)}, ...), condition=%wide.region_14.15_spmd.clone, body=%wide.region_11.14_spmd.clone.sunk | while | flops 272957440 | bytes 17481844 | solution.py:133
  283.4 2.9 fusion.122
  287.3 2.9 fusion.122
  291.1 1.0 maximum_bitcast_fusion.7
  (140 shorter events, 10.1 us)
Async XLA Ops:
  7.2 207.6 %reduce-scatter.2.cloned.1.call-start = ((), (), s32[]{:S(2)}) async-start(), calls=%async_computation.4 | async-start | bytes 2162688 | tf_op jit(solution)/shard_map/reduce_scatter | solution.py:209
  74.6 0.7 copy-start
  84.2 55.3 %copy-start.3 = (s32[2]{0:T(128)S(1)}, s32[2]{0:T(128)}, u32[]{:S(2)}) copy-start(s32[2]{0:T(128)} %constant.198) | copy-start | bytes 28
  84.2 55.4 %copy-start.4 = (s32[2]{0:T(128)S(1)}, s32[2]{0:T(128)}, u32[]{:S(2)}) copy-start(s32[2]{0:T(128)} %constant.201) | copy-start | bytes 28
  84.2 67.8 %copy-start.5 = (s32[32]{0:T(128)S(1)}, s32[32]{0:T(128)}, u32[]{:S(2)}) copy-start(s32[32]{0:T(128)} %param.17) | copy-start | bytes 388
  134.9 25.8 %copy-start.1 = (f32[2,1024]{1,0:T(2,128)S(1)}, f32[2,1024]{1,0:T(2,128)}, u32[]{:S(2)}) copy-start(f32[2,1024]{1,0:T(2,128)} %param.15) | copy-start | bytes 24580
  135.0 25.8 %copy-start.2 = (f32[2,1024]{1,0:T(2,128)S(1)}, f32[2,1024]{1,0:T(2,128)}, u32[]{:S(2)}) copy-start(f32[2,1024]{1,0:T(2,128)} %param.14) | copy-start | bytes 24580
  144.7 22.7 %all-to-all-start.1 = ((f32[1,32,64]{2,0,1:T(1,128)}), f32[1,32,64]{2,0,1:T(1,128)S(1)}, u32[]{:S(2)}, u32[]{:S(2)}) async-start(f32[1,32,64]{2,0,1:T(1,128)} %reshape.331), calls=%async_computation.1 | async-start | bytes 32768 | tf_op jit(solution)/shard_map/all_to_all | solution.py:237
  167.5 13.4 %all-to-all-start = ((f32[32,1,320]{2,1,0:T(1,128)}), f32[32,1,320]{2,1,0:T(1,128)S(1)}, u32[]{:S(2)}, u32[]{:S(2)}) async-start(f32[32,1,320]{2,1,0:T(1,128)} %reshape.432), calls=%async_computation | async-start | bytes 98304 | tf_op jit(solution)/shard_map/all_to_all | solution.py:230
  173.3 101.7 %all-gather.2.cloned.1.call-start = ((), (), s32[]{:S(2)}) async-start(), calls=%async_computation.5 | async-start | bytes 1081344 | tf_op jit(solution)/shard_map/all_gather | solution.py:266
  234.3 15.2 %all-to-all-start.2 = ((f32[32,1,128]{2,1,0:T(1,128)}), f32[32,1,128]{2,1,0:T(1,128)S(1)}, u32[]{:S(2)}, u32[]{:S(2)}) async-start(f32[32,1,128]{2,1,0:T(1,128)} %reshape.434), calls=%async_computation.3 | async-start | bytes 32768 | tf_op jit(solution)/shard_map/all_to_all | solution.py:262
Sparse Core Ops, SparseCore 0:
  74.7 140.0 reduce-scatter.1
  225.0 49.9 all-gather.1
where the time goes:
time: 300 us; the launch traced here: 299 us
  other arithmetic  110 us (37%)
  local copies, waits for them, and re-layouts  86.5 us (29%)
  waiting for transfers between devices  53.8 us (18%)
  matrix products  16.4 us (5%)
  starting transfers between devices  15.9 us (5%)
  between operations  15.2 us (5%)
    gather x11, local copies, waits for them, and re-layouts, on_device(): first_seen = jnp.searchsorted(sorted_ids, sorted_ids, side='left')  49.8 us
    convert_element_type x3, other arithmetic, phase_pair(): (jnp.sin(angles) * factor).astype(jnp.bfloat16)  31.1 us
    reduce_scatter x1, waiting for transfers between devices, on_device(): lax.psum_scatter(arranged, ('facet', 'sub'), scatter_dimension=0, tiled=T...  27 us
    all_gather x1, waiting for transfers between devices, on_device(): everything = lax.all_gather(corrected, ('facet', 'sub'), axis=0, tiled=True)  20.6 us
    neg x1, other arithmetic, column_forward(): -fine_sin  18.9 us
    concatenate x1, other arithmetic, column_adjoint(): jnp.concatenate([jnp.concatenate([fine_cos.T, -fine_sin.T], 1), jnp.conca...  12.5 us
    concatenate x1, other arithmetic, column_forward(): jnp.concatenate([jnp.concatenate([fine_cos, fine_sin], 1), jnp.concatenat...  12.2 us
    neg x1, other arithmetic, column_adjoint(): -fine_sin.T  8.58 us
  transfers between devices with their start and end apart: 5, of which 3 were waited for; matrix products, arithmetic and copies ran while one was open for 40% of the time, Pallas kernels for 0%

commit v1 on v0

v1 whole, which is shorter than its diff:
```python
import functools
import math

import jax
import jax.numpy as jnp
from jax import lax
from jax.experimental import pallas as pl
from jax.experimental.pallas import tpu as pltpu
from jax.sharding import PartitionSpec as P

N_IMG = 32768
SUBG = 64
PR_DEV = 2
VIS_BLOCK = 32
LANES = 128
CHUNK = 512

TWO_PI = 2.0 * math.pi
MESH = pl.DeviceIdType.MESH
F32 = jnp.float32
BF16 = jnp.bfloat16


def cos_sin(turns):
    quarter = jnp.floor(turns * 4.0 + 0.5)
    y = (turns - quarter * 0.25) * TWO_PI
    y2 = y * y
    s = y * (1.0 + y2 * (-1 / 6 + y2 * (1 / 120 + y2 * (-1 / 5040 + y2 * (1 / 362880)))))
    c = 1.0 + y2 * (-0.5 + y2 * (1 / 24 + y2 * (-1 / 720 + y2 * (1 / 40320))))
    k = quarter.astype(jnp.int32)
    odd = (k & 1) == 1
    cos = jnp.where(odd, s, c)
    sin = jnp.where(odd, c, s)
    cos = jnp.where(((k + 1) & 2) == 2, -cos, cos)
    sin = jnp.where((k & 2) == 2, -sin, sin)
    return cos, sin


def table(index):
    return cos_sin((index & (N_IMG - 1)).astype(F32) * (-1.0 / N_IMG))


def iota(shape, dim):
    return lax.broadcasted_iota(jnp.int32, shape, dim)


def dot(a, b):
    return jnp.dot(a, b, preferred_element_type=F32)


def dot_nt(a, b):
    return lax.dot_general(a, b, (((1,), (1,)), ((), ())), preferred_element_type=F32)


def dot_tn(a, b):
    return lax.dot_general(a, b, (((0,), (0,)), ((), ())), preferred_element_type=F32)


def three_parts(x):
    high = x.astype(BF16)
    rest = x - high.astype(F32)
    middle = rest.astype(BF16)
    low = (rest - middle.astype(F32)).astype(BF16)
    return high, middle, low


def kernel(
    facet_count,
    sub_count,
    offsets_ref,
    slab_ref,
    position_ref,
    observed_ref,
    subgrid_ref,
    clip_ref,
    adjoint_ref,
    residual_ref,
    vis_send,
    vis_recv,
    spec_send,
    spec_recv,
    back_send,
    back_recv,
    image_send,
    image_recv,
    place_ref,
    owner_ref,
    fine_one,
    fine_two,
    step_cos,
    step_sin,
    acc_ref,
    row_cos,
    row_sin,
    left_real,
    left_imag,
    basis_one,
    basis_two,
    known,
    corrected,
    send_sems,
    recv_sems,
):
    devices = facet_count * sub_count
    my_facet = lax.axis_index("facet")
    my_sub = lax.axis_index("sub")
    me = my_facet * sub_count + my_sub
    columns = sub_count
    rows = slab_ref.shape[2]
    width = slab_ref.shape[3]
    vis = position_ref.shape[1]
    row_blocks = PR_DEV * facet_count
    most = max(2, 2 * vis // (row_blocks * columns))
    span = PR_DEV * most
    group = LANES // span
    slots = devices * span
    total_rows = rows * sub_count
    tile = (8, LANES)

    def partner(i):
        other = lax.rem(me + i, devices)
        return other, (lax.div(other, sub_count), lax.rem(other, sub_count))

    barrier = pltpu.get_barrier_semaphore()

    @pl.loop(1, devices)
    def greet(i):
        unused, where = partner(i)
        pl.semaphore_signal(barrier, inc=1, device_id=where, device_id_type=MESH)

    def send_all(kind, source_of, target):
        @pl.loop(1, devices)
        def one(i):
            other, where = partner(i)
            pltpu.make_async_remote_copy(
                src_ref=source_of(other),
                dst_ref=target.at[me],
                send_sem=send_sems.at[kind],
                recv_sem=recv_sems.at[kind],
                device_id=where,
                device_id_type=MESH,
            ).start()

    def wait_all(sems, kind, target):
        whole = target.at[pl.ds(0, devices - 1)]
        pltpu.make_async_copy(whole, whole, sems.at[kind]).wait()

    ids = subgrid_ref[...].astype(F32)
    block_row = jnp.floor((ids + 0.5) * (1.0 / columns))
    block_col = ids - block_row * columns
    pair = jnp.floor((block_row + 0.5) * (1.0 / PR_DEV))
    local = block_row - pair * PR_DEV
    owner = pair * sub_count + block_col
    key = owner * PR_DEV + local
    key_rows = iota((devices * PR_DEV, vis), 0).astype(F32)
    same = jnp.where(key_rows == key, 1.0, 0.0)
    earlier = jnp.where(iota((vis, vis), 0) < iota((vis, vis), 1), 1.0, 0.0).astype(BF16)
    counts = dot(same.astype(BF16), earlier)
    rank = jnp.sum(same * counts, 0, keepdims=True)
    my_place = lax.rem(me, group) * span
    slot = my_place.astype(F32) + local * most + rank
    place = jnp.where(iota((LANES, vis), 0).astype(F32) == slot, 1.0, 0.0).astype(BF16)
    place_ref[...] = place
    owner_ref[...] = owner
    clip = jnp.broadcast_to(clip_ref[...].astype(F32), (8, clip_ref.shape[1]))
    block_start = iota((clip_ref.shape[1], vis), 0) * VIS_BLOCK
    block_at = iota((clip_ref.shape[1], vis), 1)
    in_block = (block_at >= block_start) & (block_at < block_start + VIS_BLOCK)
    spread_out = jnp.where(in_block, 1.0, 0.0).astype(BF16)
    levels = dot(clip.astype(BF16), spread_out)[0:1] * 0.25
    values = jnp.concatenate(
        [position_ref[...], observed_ref[...], levels, jnp.zeros((3, vis), F32)], 0
    )
    chosen = iota((devices, 8, vis), 0).astype(F32) == owner[None]
    packed = jnp.zeros((devices * 8, LANES), F32)
    for part in three_parts(values):
        masked = jnp.where(chosen, part.astype(F32)[None], 0.0)
        masked = masked.reshape(devices * 8, vis).astype(BF16)
        packed = packed + dot_nt(masked, place)
    row_offset = offsets_ref[0, 0].astype(F32)
    packed = packed.reshape(devices, 8, LANES)
    packed = jnp.where(iota((devices, 8, LANES), 1) == 5, row_offset, packed)
    vis_send[...] = packed
    vis_recv[me] = vis_send[me]

    pl.semaphore_wait(barrier, devices - 1)
    send_all(0, lambda other: vis_send.at[other], vis_recv)

    col_offset = offsets_ref[0, 1]
    lane = iota((LANES, LANES), 1)
    tone = lane & (SUBG - 1)
    first_half = lane < SUBG
    base_cos, base_sin = table((col_offset + iota((LANES, LANES), 0)) * tone)
    scale = width ** (-0.5)
    base_one = jnp.where(first_half, base_cos, base_sin) * scale
    base_two = jnp.where(first_half, -base_sin, base_cos) * scale
    step_count = width // LANES
    step_tone = iota((step_count, LANES), 1) & (SUBG - 1)
    sc, ss = table(iota((step_count, LANES), 0) * LANES * step_tone)
    step_cos[...] = sc
    step_sin[...] = ss
    coarse_step = N_IMG // columns
    coarse_at = col_offset + iota((columns, LANES), 1)
    coarse_index = ((coarse_at & (columns - 1)) * iota((columns, LANES), 0)) * coarse_step
    coarse_cos, coarse_sin = table(coarse_index)
    coarse_cos = coarse_cos.astype(BF16).astype(F32)
    coarse_sin = coarse_sin.astype(BF16).astype(F32)
    copies = CHUNK // LANES
    wide_cos = jnp.concatenate([coarse_cos] * copies, 1)
    wide_sin = jnp.concatenate([coarse_sin] * copies, 1)
    acc_ref[...] = jnp.zeros_like(acc_ref)

    @pl.loop(0, width // CHUNK)
    def forward(c):
        at = pl.multiple_of(c * CHUNK, CHUNK)
        ones, twos = [], []
        for k in range(copies):
            ca = step_cos[pl.ds(c * copies + k, 1), :]
            sa = step_sin[pl.ds(c * copies + k, 1), :]
            ones.append((ca * base_one + sa * base_two).astype(BF16))
            twos.append((ca * base_two - sa * base_one).astype(BF16))
        one = jnp.concatenate(ones, 0)
        two = jnp.concatenate(twos, 0)
        fine_one[pl.ds(at, CHUNK), :] = one
        fine_two[pl.ds(at, CHUNK), :] = two
        real = slab_ref[0, 0, :, pl.ds(at, CHUNK)].astype(F32)
        imag = slab_ref[0, 1, :, pl.ds(at, CHUNK)].astype(F32)
        mod_real, mod_imag = [], []
        for q in range(columns):
            cc = wide_cos[q : q + 1]
            cs = wide_sin[q : q + 1]
            mod_real.append((real * cc - imag * cs).astype(BF16))
            mod_imag.append((real * cs + imag * cc).astype(BF16))
        acc_ref[...] += dot(jnp.concatenate(mod_real, 0), one) + dot(
            jnp.concatenate(mod_imag, 0), two
        )

    spec_send[...] = acc_ref[...].astype(BF16).reshape(columns, rows, LANES)
    spec_recv[me] = spec_send[my_sub]
    send_all(1, lambda other: spec_send.at[lax.rem(other, sub_count)], spec_recv)

    wait_all(recv_sems, 0, vis_recv)
    table_lane = iota((total_rows, LANES), 1)
    table_block = PR_DEV * my_facet + (table_lane >= SUBG).astype(jnp.int32)
    row_tone = table_block * (N_IMG // row_blocks) + (table_lane & (SUBG - 1))
    row_scale = 0.5 * total_rows ** (-0.5)
    for f in range(facet_count):
        start = vis_recv[f * sub_count][5:6, :].astype(jnp.int32)
        rc, rs = table((start + iota((total_rows, LANES), 0)) * row_tone)
        row_cos[pl.ds(f * total_rows, total_rows), :] = (rc * row_scale).astype(BF16)
        row_sin[pl.ds(f * total_rows, total_rows), :] = (rs * row_scale).astype(BF16)
    for j in range(slots // LANES):
        merged = vis_recv[j * group]
        for i in range(1, group):
            merged = merged + vis_recv[j * group + i]
        known[:, j * LANES : (j + 1) * LANES] = merged

    factor = SUBG ** (-0.5)

    @pl.loop(0, slots // CHUNK)
    def bases(c):
        at = pl.ds(pl.multiple_of(c * CHUNK, CHUNK), CHUNK)
        grid = iota((SUBG, CHUNK), 0).astype(F32) * (1.0 / SUBG)
        lr, li = cos_sin(known[0:1, at] * grid)
        left_real[:, at] = lr * factor
        left_imag[:, at] = li * factor
        rr, ri = cos_sin(known[1:2, at] * grid)
        rr = rr * factor
        ri = ri * factor
        basis_one[:, at] = jnp.concatenate([rr, -ri], 0).astype(BF16)
        basis_two[:, at] = jnp.concatenate([ri, rr], 0).astype(BF16)

    wait_all(recv_sems, 1, spec_recv)
    spectra = spec_recv[...].reshape(facet_count * total_rows, LANES).astype(F32)
    half = iota((1, LANES), 1) < SUBG
    turned = pltpu.roll(spectra, SUBG, 1)
    turned = jnp.where(half, -turned, turned)
    subgrids = dot_tn(row_cos[...], spectra.astype(BF16)) + dot_tn(
        row_sin[...], turned.astype(BF16)
    )
    subgrids = subgrids.astype(BF16)
    acc_out = jnp.zeros((LANES, LANES), F32)
    for c in range(slots // CHUNK):
        at = slice(c * CHUNK, (c + 1) * CHUNK)
        lr = left_real[:, at]
        li = left_imag[:, at]
        one = basis_one[:, at]
        two = basis_two[:, at]
        slot_lane = iota((1, CHUNK), 1) & (span - 1)
        second = slot_lane >= most
        inner_real = dot(subgrids, one)
        inner_imag = dot(subgrids, two)
        inner_real = jnp.where(second, inner_real[SUBG:], inner_real[:SUBG])
        inner_imag = jnp.where(second, inner_imag[SUBG:], inner_imag[:SUBG])
        level = known[4:5, at]
        live = jnp.where(level > 0.0, 1.0, 0.0)
        misfit_real = known[2:3, at] - jnp.sum(lr * inner_real - li * inner_imag, 0, keepdims=True)
        misfit_imag = known[3:4, at] - jnp.sum(lr * inner_imag + li * inner_real, 0, keepdims=True)
        threshold = level + (1.0 - live)
        magnitude = jnp.sqrt(misfit_real * misfit_real + misfit_imag * misfit_imag)
        weight = live * threshold / jnp.maximum(magnitude, threshold)
        wr = weight * misfit_real
        wi = weight * misfit_imag
        blank = jnp.zeros((6, LANES), F32)
        for k in range(copies):
            part = slice(k * LANES, (k + 1) * LANES)
            back_send[c * copies + k] = jnp.concatenate([wr[:, part], wi[:, part], blank], 0)
        pr = lr * wr + li * wi
        pi = lr * wi - li * wr
        pr = jnp.concatenate([jnp.where(second, 0.0, pr), jnp.where(second, pr, 0.0)], 0)
        pi = jnp.concatenate([jnp.where(second, 0.0, pi), jnp.where(second, pi, 0.0)], 0)
        acc_out = acc_out + dot_nt(pr.astype(BF16), one) + dot_nt(pi.astype(BF16), two)
    back_recv[me] = back_send[lax.div(me, group)]
    send_all(2, lambda other: back_send.at[lax.div(other, group)], back_recv)

    corrected[...] = acc_out.astype(BF16)
    gridded = corrected[...].astype(F32)
    turned = pltpu.roll(gridded, SUBG, 1)
    turned = jnp.where(half, turned, -turned)
    parts = dot(row_cos[...], gridded.astype(BF16)) + dot(row_sin[...], turned.astype(BF16))
    image_send[...] = parts.astype(BF16).reshape(devices, rows, LANES)
    image_recv[me] = image_send[me]
    send_all(3, lambda other: image_send.at[other], image_recv)

    wait_all(recv_sems, 2, back_recv)
    returned = back_recv[...].reshape(devices * 8, LANES)
    found = jnp.zeros((devices * 8, vis), F32)
    for part in three_parts(returned):
        found = found + dot(part, place_ref[...])
    chosen = iota((devices, 8, vis), 0).astype(F32) == owner_ref[...][None]
    found = jnp.sum(jnp.where(chosen, found.reshape(devices, 8, vis), 0.0), 0)
    residual_ref[...] = found[0:2]

    wait_all(recv_sems, 3, image_recv)
    held = image_recv[...].astype(F32).reshape(facet_count, columns * rows, LANES)
    images = held[0]
    for f in range(1, facet_count):
        images = images + held[f]
    images = images.astype(BF16)

    @pl.loop(0, width // CHUNK)
    def adjoint(c):
        at = pl.ds(pl.multiple_of(c * CHUNK, CHUNK), CHUNK)
        real = dot_nt(images, fine_one[at, :])
        imag = dot_nt(images, fine_two[at, :])
        out_real = jnp.zeros((rows, CHUNK), F32)
        out_imag = jnp.zeros((rows, CHUNK), F32)
        for q in range(columns):
            cc = wide_cos[q : q + 1]
            cs = wide_sin[q : q + 1]
            sr = real[q * rows : (q + 1) * rows]
            si = imag[q * rows : (q + 1) * rows]
            out_real = out_real + (cc * sr + cs * si)
            out_imag = out_imag + (cc * si - cs * sr)
        adjoint_ref[0, 0, :, at] = out_real
        adjoint_ref[0, 1, :, at] = out_imag

    wait_all(send_sems, 0, vis_recv)
    wait_all(send_sems, 1, spec_recv)
    wait_all(send_sems, 2, back_recv)
    wait_all(send_sems, 3, image_recv)


def on_device(
    facet_slab, facet_offsets, visibility_position, observed, visibility_subgrid, clip_levels
):
    sub_count = lax.axis_size("sub")
    facet_count = lax.axis_size("facet")
    devices = sub_count * facet_count
    rows = facet_slab.shape[2]
    width = facet_slab.shape[3]
    vis = visibility_position.shape[1]
    most = max(2, 2 * vis // (PR_DEV * facet_count * sub_count))
    slots = devices * PR_DEV * most
    all_rows = devices * rows
    vmem = pl.BlockSpec(memory_space=pltpu.VMEM)
    smem = pl.BlockSpec(memory_space=pltpu.SMEM)
    return pl.pallas_call(
        functools.partial(kernel, facet_count, sub_count),
        out_shape=(
            jax.ShapeDtypeStruct(facet_slab.shape, F32),
            jax.ShapeDtypeStruct((2, vis), F32),
        ),
        in_specs=[smem] + [vmem] * 5,
        out_specs=(vmem, vmem),
        scratch_shapes=[
            pltpu.VMEM((devices, 8, LANES), F32),
            pltpu.VMEM((devices, 8, LANES), F32),
            pltpu.VMEM((sub_count, rows, LANES), BF16),
            pltpu.VMEM((devices, rows, LANES), BF16),
            pltpu.VMEM((slots // LANES, 8, LANES), F32),
            pltpu.VMEM((devices, 8, LANES), F32),
            pltpu.VMEM((devices, rows, LANES), BF16),
            pltpu.VMEM((devices, rows, LANES), BF16),
            pltpu.VMEM((LANES, vis), BF16),
            pltpu.VMEM((1, vis), F32),
            pltpu.VMEM((width, LANES), BF16),
            pltpu.VMEM((width, LANES), BF16),
            pltpu.VMEM((width // LANES, LANES), F32),
            pltpu.VMEM((width // LANES, LANES), F32),
            pltpu.VMEM((sub_count * rows, LANES), F32),
            pltpu.VMEM((all_rows, LANES), BF16),
            pltpu.VMEM((all_rows, LANES), BF16),
            pltpu.VMEM((SUBG, slots), F32),
            pltpu.VMEM((SUBG, slots), F32),
            pltpu.VMEM((2 * SUBG, slots), BF16),
            pltpu.VMEM((2 * SUBG, slots), BF16),
            pltpu.VMEM((8, slots), F32),
            pltpu.VMEM((LANES, LANES), BF16),
            pltpu.SemaphoreType.DMA((4,)),
            pltpu.SemaphoreType.DMA((4,)),
        ],
        compiler_params=pltpu.CompilerParams(
            collective_id=0, has_side_effects=True, vmem_limit_bytes=56 * 1024 * 1024
        ),
    )(
        facet_offsets,
        facet_slab,
        visibility_position,
        observed,
        visibility_subgrid.reshape(1, vis),
        clip_levels.reshape(1, -1),
    )


def solution(mesh):
    placed = (
        P("facet", None, "sub", None),
        P("facet", None),
        P(None, ("facet", "sub")),
        P(None, ("facet", "sub")),
        P(("facet", "sub"), None),
        P(("facet", "sub")),
    )
    return jax.shard_map(
        on_device,
        mesh=mesh,
        in_specs=placed,
        out_specs=(P("facet", None, "sub", None), P(None, ("facet", "sub"))),
        check_vma=False,
    )
```

time: 300 us -> 36.5 us (0.12)
  other arithmetic: 110 us -> 0 us
  local copies, waits for them, and re-layouts: 86.5 us -> 2.87 us
  waiting for transfers between devices: 53.8 us -> 0 us
  Pallas kernels: 0 us -> 32.9 us
  matrix products: 16.4 us -> 0 us
  starting transfers between devices: 15.9 us -> 0 us
  between operations: 15.2 us -> 0.65 us
    gather x13 -> x0, local copies, waits for them, and re-layouts: 57.1 us -> none  [the longest x11 49.8 us: on_device(): first_seen = jnp.searchsorted(sorted_ids, sorted_ids, side='left')]
    convert_element_type x16 -> x0, other arithmetic: 38.8 us -> none  [the longest x3 31.1 us: phase_pair(): (jnp.sin(angles) * factor).astype(jnp.bfloat16)]
    pallas_call x0 -> x1, Pallas kernels: none -> 32.9 us  [on_device(): pl.pallas_call(functools.partial(kernel, facet_count, sub_count), out_sha...]
    neg x4 -> x0, other arithmetic: 29.5 us -> none  [the longest x1 18.9 us: column_forward(): -fine_sin]
    reduce_scatter x1 -> x0, waiting for transfers between devices: 27 us -> none  [on_device(): lax.psum_scatter(arranged, ('facet', 'sub'), scatter_dimension=0, tiled=T...]
    concatenate x5 -> x0, other arithmetic: 26.5 us -> none  [the longest x1 12.5 us: column_adjoint(): jnp.concatenate([jnp.concatenate([fine_cos.T, -fine_sin.T], 1), jnp.conca...]
    all_gather x1 -> x0, waiting for transfers between devices: 20.6 us -> none  [on_device(): everything = lax.all_gather(corrected, ('facet', 'sub'), axis=0, tiled=True)]
    dot_general x12 -> x0, matrix products: 16.4 us -> none  [the longest x2 6.13 us: one_group(): jnp.dot(joined, forward_matrix, preferred_element_type=jnp.float32)]
  transfers between devices with their start and end apart: 5 -> 0, of which waited for: 3 -> 0; matrix products, arithmetic and copies ran while one was open for 40% -> 0% of each run, Pallas kernels for 0% -> 0%
where the time goes in v1:
time: 36.5 us; the launch traced here: 36.4 us
  Pallas kernels  32.9 us (90%)
  local copies, waits for them, and re-layouts  2.87 us (8%)
  between operations  0.65 us (2%)
    pallas_call x1, Pallas kernels, on_device(): pl.pallas_call(functools.partial(kernel, facet_count, sub_count), out_sha...  32.9 us
    unnamed x4, local copies, waits for them, and re-layouts  2.87 us

profile of v1, /device:TPU:0, one launch (start us, length us, event | category | flops | bytes accessed | tf_op | source)
XLA Modules:
  0.0 36.4 jit_solution(3421172604484558119)
XLA Ops:
  0.6 32.9 %shard_map.77 = (f32[1,2,16,8192]{3,2,1,0:T(8,128)}, f32[2,1024]{1,0:T(2,128)}) custom-call(s32[1,2]{1,0:T(1,128)} %offsets_ref.1, bf16[1,2,16,8192]{3,2,1,0:T(8,128)(2,1)} %slab_ref.1, f32[2,1024]{1,0:T(2,128)} %position_ref.1, f32[2,1024]{1,0:T(2,128)} %observed_ref.1, s32[1,1024]{1,0:T(1,128)} %bitcast.2, s32[1,32]{1,0:T(1,128)} %bitcast.3), custom_call_target="tpu_custom_call" | custom-call | tf_op jit(solution)/shard_map/pallas_call | solution.py:378
  33.5 0.0 copy-start
  33.5 2.3 %copy.10 = f32[1,2,16,8192]{3,2,1,0:T(8,128)} copy(f32[1,2,16,8192]{3,2,1,0:T(8,128)} %get-tuple-element.4) | data formatting | bytes 2097152
  35.8 0.0 copy-done
  35.8 0.6 %copy.11 = f32[2,1024]{1,0:T(2,128)} copy(f32[2,1024]{1,0:T(2,128)S(1)} %copy-done) | data formatting | bytes 16384
Async XLA Ops:
  33.5 2.3 %copy-start = (f32[2,1024]{1,0:T(2,128)S(1)}, f32[2,1024]{1,0:T(2,128)}, u32[]{:S(2)}) copy-start(f32[2,1024]{1,0:T(2,128)} %get-tuple-element.5) | copy-start | bytes 24580

commit v2 on v1

--- a/solution.py
+++ b/solution.py
@@ -64,6 +64,29 @@
     return high, middle, low
 
 
+def column_tables(col_offset, columns, width, matrix_ref, step_cos, step_sin):
+    lane = iota((LANES, LANES), 1)
+    first_half = lane < SUBG
+    base_cos, base_sin = table((col_offset + iota((LANES, LANES), 0)) * (lane & (SUBG - 1)))
+    scale = width ** (-0.5)
+    base_one = jnp.where(first_half, base_cos, base_sin) * scale
+    base_two = jnp.where(first_half, -base_sin, base_cos) * scale
+    coarse_step = N_IMG // columns
+    residue = (col_offset + iota((columns, LANES), 0)) & (columns - 1)
+    for q in range(columns):
+        cc, cs = table(residue * (q * coarse_step))
+        cc = jnp.concatenate([cc] * (LANES // columns), 0)
+        cs = jnp.concatenate([cs] * (LANES // columns), 0)
+        at = slice(q * LANES, (q + 1) * LANES)
+        matrix_ref[:LANES, at] = (cc * base_one + cs * base_two).astype(BF16)
+        matrix_ref[LANES:, at] = (cc * base_two - cs * base_one).astype(BF16)
+    steps = width // LANES
+    step_lane = iota((steps, LANES), 1)
+    sc, ss = table(iota((steps, LANES), 0) * LANES * (step_lane & (SUBG - 1)))
+    step_cos[...] = sc
+    step_sin[...] = jnp.where(step_lane < SUBG, ss, -ss)
+
+
 def kernel(
     facet_count,
     sub_count,
@@ -73,7 +96,7 @@
     observed_ref,
     subgrid_ref,
     clip_ref,
-    adjoint_ref,
+    image_ref,
     residual_ref,
     vis_send,
     vis_recv,
@@ -85,19 +108,17 @@
     image_recv,
     place_ref,
     owner_ref,
-    fine_one,
-    fine_two,
+    slab_rows,
+    matrix,
     step_cos,
     step_sin,
-    acc_ref,
-    row_cos,
-    row_sin,
+    row_wide,
+    row_tall,
     left_real,
     left_imag,
     basis_one,
     basis_two,
     known,
-    corrected,
     send_sems,
     recv_sems,
 ):
@@ -115,29 +136,29 @@
     group = LANES // span
     slots = devices * span
     total_rows = rows * sub_count
-    tile = (8, LANES)
-
-    def partner(i):
-        other = lax.rem(me + i, devices)
-        return other, (lax.div(other, sub_count), lax.rem(other, sub_count))
+
+    partners = []
+    for df in range(facet_count):
+        facet = my_facet + df
+        facet = jnp.where(facet >= facet_count, facet - facet_count, facet)
+        for ds in range(sub_count):
+            sub = my_sub + ds
+            sub = jnp.where(sub >= sub_count, sub - sub_count, sub)
+            if df or ds:
+                partners.append((facet, sub))
 
     barrier = pltpu.get_barrier_semaphore()
-
-    @pl.loop(1, devices)
-    def greet(i):
-        unused, where = partner(i)
+    for where in partners:
         pl.semaphore_signal(barrier, inc=1, device_id=where, device_id_type=MESH)
 
     def send_all(kind, source_of, target):
-        @pl.loop(1, devices)
-        def one(i):
-            other, where = partner(i)
+        for facet, sub in partners:
             pltpu.make_async_remote_copy(
-                src_ref=source_of(other),
+                src_ref=source_of(facet, sub),
                 dst_ref=target.at[me],
                 send_sem=send_sems.at[kind],
                 recv_sem=recv_sems.at[kind],
-                device_id=where,
+                device_id=(facet, sub),
                 device_id_type=MESH,
             ).start()
 
@@ -154,9 +175,15 @@
     key = owner * PR_DEV + local
     key_rows = iota((devices * PR_DEV, vis), 0).astype(F32)
     same = jnp.where(key_rows == key, 1.0, 0.0)
-    earlier = jnp.where(iota((vis, vis), 0) < iota((vis, vis), 1), 1.0, 0.0).astype(BF16)
-    counts = dot(same.astype(BF16), earlier)
-    rank = jnp.sum(same * counts, 0, keepdims=True)
+    earlier = jnp.where(iota((LANES, LANES), 0) < iota((LANES, LANES), 1), 1.0, 0.0).astype(BF16)
+    before = jnp.zeros((devices * PR_DEV, 1), F32)
+    ranks = []
+    for k in range(vis // LANES):
+        block = same[:, k * LANES : (k + 1) * LANES]
+        counts = dot(block.astype(BF16), earlier) + before
+        ranks.append(jnp.sum(block * counts, 0, keepdims=True))
+        before = before + jnp.sum(block, 1, keepdims=True)
+    rank = jnp.concatenate(ranks, 1)
     my_place = lax.rem(me, group) * span
     slot = my_place.astype(F32) + local * most + rank
     place = jnp.where(iota((LANES, vis), 0).astype(F32) == slot, 1.0, 0.0).astype(BF16)
@@ -184,60 +211,36 @@
     vis_recv[me] = vis_send[me]
 
     pl.semaphore_wait(barrier, devices - 1)
-    send_all(0, lambda other: vis_send.at[other], vis_recv)
-
-    col_offset = offsets_ref[0, 1]
-    lane = iota((LANES, LANES), 1)
-    tone = lane & (SUBG - 1)
-    first_half = lane < SUBG
-    base_cos, base_sin = table((col_offset + iota((LANES, LANES), 0)) * tone)
-    scale = width ** (-0.5)
-    base_one = jnp.where(first_half, base_cos, base_sin) * scale
-    base_two = jnp.where(first_half, -base_sin, base_cos) * scale
-    step_count = width // LANES
-    step_tone = iota((step_count, LANES), 1) & (SUBG - 1)
-    sc, ss = table(iota((step_count, LANES), 0) * LANES * step_tone)
-    step_cos[...] = sc
-    step_sin[...] = ss
-    coarse_step = N_IMG // columns
-    coarse_at = col_offset + iota((columns, LANES), 1)
-    coarse_index = ((coarse_at & (columns - 1)) * iota((columns, LANES), 0)) * coarse_step
-    coarse_cos, coarse_sin = table(coarse_index)
-    coarse_cos = coarse_cos.astype(BF16).astype(F32)
-    coarse_sin = coarse_sin.astype(BF16).astype(F32)
-    copies = CHUNK // LANES
-    wide_cos = jnp.concatenate([coarse_cos] * copies, 1)
-    wide_sin = jnp.concatenate([coarse_sin] * copies, 1)
-    acc_ref[...] = jnp.zeros_like(acc_ref)
-
-    @pl.loop(0, width // CHUNK)
-    def forward(c):
-        at = pl.multiple_of(c * CHUNK, CHUNK)
-        ones, twos = [], []
-        for k in range(copies):
-            ca = step_cos[pl.ds(c * copies + k, 1), :]
-            sa = step_sin[pl.ds(c * copies + k, 1), :]
-            ones.append((ca * base_one + sa * base_two).astype(BF16))
-            twos.append((ca * base_two - sa * base_one).astype(BF16))
-        one = jnp.concatenate(ones, 0)
-        two = jnp.concatenate(twos, 0)
-        fine_one[pl.ds(at, CHUNK), :] = one
-        fine_two[pl.ds(at, CHUNK), :] = two
-        real = slab_ref[0, 0, :, pl.ds(at, CHUNK)].astype(F32)
-        imag = slab_ref[0, 1, :, pl.ds(at, CHUNK)].astype(F32)
-        mod_real, mod_imag = [], []
-        for q in range(columns):
-            cc = wide_cos[q : q + 1]
-            cs = wide_sin[q : q + 1]
-            mod_real.append((real * cc - imag * cs).astype(BF16))
-            mod_imag.append((real * cs + imag * cc).astype(BF16))
-        acc_ref[...] += dot(jnp.concatenate(mod_real, 0), one) + dot(
-            jnp.concatenate(mod_imag, 0), two
-        )
-
-    spec_send[...] = acc_ref[...].astype(BF16).reshape(columns, rows, LANES)
+    send_all(0, lambda f, s: vis_send.at[f * sub_count + s], vis_recv)
+
+    column_tables(offsets_ref[0, 1], columns, width, matrix, step_cos, step_sin)
+    steps = width // LANES
+    for h in range(steps):
+        part = slice(h * LANES, (h + 1) * LANES)
+        for c in range(2):
+            slab_rows[h * rows : (h + 1) * rows, c * LANES : (c + 1) * LANES] = slab_ref[
+                0, c, :, part
+            ]
+    taken = 16
+    for q in range(0, columns, 2):
+        both = matrix[:, q * LANES : (q + 2) * LANES]
+        straight = jnp.zeros((rows, 2 * LANES), F32)
+        crossed = jnp.zeros((rows, 2 * LANES), F32)
+        for h in range(0, steps, taken):
+            spread = dot(slab_rows[h * rows : (h + taken) * rows, :], both)
+            for k in range(taken):
+                piece = spread[k * rows : (k + 1) * rows]
+                sc = step_cos[h + k : h + k + 1, :]
+                ss = step_sin[h + k : h + k + 1, :]
+                straight = straight + piece * jnp.concatenate([sc, sc], 1)
+                crossed = crossed + piece * jnp.concatenate([ss, ss], 1)
+        for k in range(2):
+            part = slice(k * LANES, (k + 1) * LANES)
+            spectrum = straight[:, part] + pltpu.roll(crossed[:, part], SUBG, 1)
+            spec_send[q + k] = spectrum.astype(BF16)
+
     spec_recv[me] = spec_send[my_sub]
-    send_all(1, lambda other: spec_send.at[lax.rem(other, sub_count)], spec_recv)
+    send_all(1, lambda f, s: spec_send.at[s], spec_recv)
 
     wait_all(recv_sems, 0, vis_recv)
     table_lane = iota((total_rows, LANES), 1)
@@ -247,8 +250,13 @@
     for f in range(facet_count):
         start = vis_recv[f * sub_count][5:6, :].astype(jnp.int32)
         rc, rs = table((start + iota((total_rows, LANES), 0)) * row_tone)
-        row_cos[pl.ds(f * total_rows, total_rows), :] = (rc * row_scale).astype(BF16)
-        row_sin[pl.ds(f * total_rows, total_rows), :] = (rs * row_scale).astype(BF16)
+        rc = rc * row_scale
+        rs = rs * row_scale
+        at = slice(f * total_rows, (f + 1) * total_rows)
+        row_wide[at, :LANES] = rc.astype(BF16)
+        row_wide[at, LANES:] = rs.astype(BF16)
+        row_tall[:LANES, at] = rc.T.astype(BF16)
+        row_tall[LANES:, at] = rs.T.astype(BF16)
     for j in range(slots // LANES):
         merged = vis_recv[j * group]
         for i in range(1, group):
@@ -271,15 +279,14 @@
         basis_two[:, at] = jnp.concatenate([ri, rr], 0).astype(BF16)
 
     wait_all(recv_sems, 1, spec_recv)
-    spectra = spec_recv[...].reshape(facet_count * total_rows, LANES).astype(F32)
+    spectra = spec_recv[...].reshape(facet_count * total_rows, LANES)
+    both = dot(row_tall[...], spectra)
     half = iota((1, LANES), 1) < SUBG
-    turned = pltpu.roll(spectra, SUBG, 1)
-    turned = jnp.where(half, -turned, turned)
-    subgrids = dot_tn(row_cos[...], spectra.astype(BF16)) + dot_tn(
-        row_sin[...], turned.astype(BF16)
-    )
+    turned = pltpu.roll(both[LANES:], SUBG, 1)
+    subgrids = both[:LANES] + jnp.where(half, -turned, turned)
     subgrids = subgrids.astype(BF16)
     acc_out = jnp.zeros((LANES, LANES), F32)
+    copies = CHUNK // LANES
     for c in range(slots // CHUNK):
         at = slice(c * CHUNK, (c + 1) * CHUNK)
         lr = left_real[:, at]
@@ -310,17 +317,17 @@
         pr = jnp.concatenate([jnp.where(second, 0.0, pr), jnp.where(second, pr, 0.0)], 0)
         pi = jnp.concatenate([jnp.where(second, 0.0, pi), jnp.where(second, pi, 0.0)], 0)
         acc_out = acc_out + dot_nt(pr.astype(BF16), one) + dot_nt(pi.astype(BF16), two)
-    back_recv[me] = back_send[lax.div(me, group)]
-    send_all(2, lambda other: back_send.at[lax.div(other, group)], back_recv)
-
-    corrected[...] = acc_out.astype(BF16)
-    gridded = corrected[...].astype(F32)
+
+    gridded = acc_out.astype(BF16).astype(F32)
     turned = pltpu.roll(gridded, SUBG, 1)
     turned = jnp.where(half, turned, -turned)
-    parts = dot(row_cos[...], gridded.astype(BF16)) + dot(row_sin[...], turned.astype(BF16))
+    gridded = jnp.concatenate([gridded, turned], 0).astype(BF16)
+    parts = dot(row_wide[...], gridded)
     image_send[...] = parts.astype(BF16).reshape(devices, rows, LANES)
+    send_all(3, lambda f, s: image_send.at[f * sub_count + s], image_recv)
+    send_all(2, lambda f, s: back_send.at[lax.div(f * sub_count + s, group)], back_recv)
     image_recv[me] = image_send[me]
-    send_all(3, lambda other: image_send.at[other], image_recv)
+    back_recv[me] = back_send[lax.div(me, group)]
 
     wait_all(recv_sems, 2, back_recv)
     returned = back_recv[...].reshape(devices * 8, LANES)
@@ -336,29 +343,56 @@
     images = held[0]
     for f in range(1, facet_count):
         images = images + held[f]
-    images = images.astype(BF16)
-
-    @pl.loop(0, width // CHUNK)
-    def adjoint(c):
-        at = pl.ds(pl.multiple_of(c * CHUNK, CHUNK), CHUNK)
-        real = dot_nt(images, fine_one[at, :])
-        imag = dot_nt(images, fine_two[at, :])
-        out_real = jnp.zeros((rows, CHUNK), F32)
-        out_imag = jnp.zeros((rows, CHUNK), F32)
-        for q in range(columns):
-            cc = wide_cos[q : q + 1]
-            cs = wide_sin[q : q + 1]
-            sr = real[q * rows : (q + 1) * rows]
-            si = imag[q * rows : (q + 1) * rows]
-            out_real = out_real + (cc * sr + cs * si)
-            out_imag = out_imag + (cc * si - cs * sr)
-        adjoint_ref[0, 0, :, at] = out_real
-        adjoint_ref[0, 1, :, at] = out_imag
+    image_ref[...] = images
 
     wait_all(send_sems, 0, vis_recv)
     wait_all(send_sems, 1, spec_recv)
     wait_all(send_sems, 2, back_recv)
     wait_all(send_sems, 3, image_recv)
+
+
+def adjoint_kernel(
+    columns,
+    width,
+    offsets_ref,
+    image_ref,
+    found_ref,
+    adjoint_ref,
+    residual_ref,
+    matrix,
+    step_cos,
+    step_sin,
+    straight,
+    crossed,
+):
+    rows = adjoint_ref.shape[2]
+    block_steps = adjoint_ref.shape[3] // LANES
+
+    @pl.when(pl.program_id(0) == 0)
+    def first():
+        residual_ref[...] = found_ref[...]
+        column_tables(offsets_ref[0, 1], columns, width, matrix, step_cos, step_sin)
+        for q in range(columns):
+            image = image_ref[q * rows : (q + 1) * rows, :]
+            at = slice(q * LANES, (q + 1) * LANES)
+            straight[:, at] = image
+            crossed[:, at] = pltpu.roll(image, SUBG, 1)
+
+    start = pl.program_id(0) * block_steps
+    pieces = []
+    for h in range(block_steps):
+        sc = step_cos[pl.ds(start + h, 1), :]
+        ss = step_sin[pl.ds(start + h, 1), :]
+        piece = []
+        for q in range(columns):
+            at = slice(q * LANES, (q + 1) * LANES)
+            piece.append((straight[:, at] * sc + crossed[:, at] * ss).astype(BF16))
+        pieces.append(jnp.concatenate(piece, 1))
+    out = dot_nt(jnp.concatenate(pieces, 0), matrix[...])
+    for h in range(block_steps):
+        at = slice(h * LANES, (h + 1) * LANES)
+        adjoint_ref[0, 0, :, at] = out[h * rows : (h + 1) * rows, :LANES]
+        adjoint_ref[0, 1, :, at] = out[h * rows : (h + 1) * rows, LANES:]
 
 
 def on_device(
@@ -375,10 +409,10 @@
     all_rows = devices * rows
     vmem = pl.BlockSpec(memory_space=pltpu.VMEM)
     smem = pl.BlockSpec(memory_space=pltpu.SMEM)
-    return pl.pallas_call(
+    images, found = pl.pallas_call(
         functools.partial(kernel, facet_count, sub_count),
         out_shape=(
-            jax.ShapeDtypeStruct(facet_slab.shape, F32),
+            jax.ShapeDtypeStruct((sub_count * rows, LANES), F32),
             jax.ShapeDtypeStruct((2, vis), F32),
         ),
         in_specs=[smem] + [vmem] * 5,
@@ -394,19 +428,17 @@
             pltpu.VMEM((devices, rows, LANES), BF16),
             pltpu.VMEM((LANES, vis), BF16),
             pltpu.VMEM((1, vis), F32),
-            pltpu.VMEM((width, LANES), BF16),
-            pltpu.VMEM((width, LANES), BF16),
+            pltpu.VMEM((width // LANES * rows, 2 * LANES), BF16),
+            pltpu.VMEM((2 * LANES, sub_count * LANES), BF16),
             pltpu.VMEM((width // LANES, LANES), F32),
             pltpu.VMEM((width // LANES, LANES), F32),
-            pltpu.VMEM((sub_count * rows, LANES), F32),
-            pltpu.VMEM((all_rows, LANES), BF16),
-            pltpu.VMEM((all_rows, LANES), BF16),
+            pltpu.VMEM((all_rows, 2 * LANES), BF16),
+            pltpu.VMEM((2 * LANES, all_rows), BF16),
             pltpu.VMEM((SUBG, slots), F32),
             pltpu.VMEM((SUBG, slots), F32),
             pltpu.VMEM((2 * SUBG, slots), BF16),
             pltpu.VMEM((2 * SUBG, slots), BF16),
             pltpu.VMEM((8, slots), F32),
-            pltpu.VMEM((LANES, LANES), BF16),
             pltpu.SemaphoreType.DMA((4,)),
             pltpu.SemaphoreType.DMA((4,)),
         ],
@@ -421,6 +453,29 @@
         visibility_subgrid.reshape(1, vis),
         clip_levels.reshape(1, -1),
     )
+    blocks = 4
+    whole = lambda *shape: pl.BlockSpec(shape, lambda i: (0,) * len(shape))
+    return pl.pallas_call(
+        functools.partial(adjoint_kernel, sub_count, width),
+        grid=(blocks,),
+        out_shape=(
+            jax.ShapeDtypeStruct(facet_slab.shape, F32),
+            jax.ShapeDtypeStruct((2, vis), F32),
+        ),
+        in_specs=[smem, whole(sub_count * rows, LANES), whole(2, vis)],
+        out_specs=(
+            pl.BlockSpec((1, 2, rows, width // blocks), lambda i: (0, 0, 0, i)),
+            whole(2, vis),
+        ),
+        scratch_shapes=[
+            pltpu.VMEM((2 * LANES, sub_count * LANES), BF16),
+            pltpu.VMEM((width // LANES, LANES), F32),
+            pltpu.VMEM((width // LANES, LANES), F32),
+            pltpu.VMEM((rows, sub_count * LANES), F32),
+            pltpu.VMEM((rows, sub_count * LANES), F32),
+        ],
+        compiler_params=pltpu.CompilerParams(vmem_limit_bytes=32 * 1024 * 1024),
+    )(facet_offsets, images, found)
 
 
 def solution(mesh):

time: 36.5 us -> 33.9 us (0.929)
  Pallas kernels: 32.9 us -> 30.9 us
  local copies, waits for them, and re-layouts: 2.87 us -> 2.19 us
    pallas_call x1, Pallas kernels: 32.9 us -> 27.4 us  [on_device(): pl.pallas_call(functools.partial(kernel, facet_count, sub_count), out_sha...]
    pallas_call x0 -> x1, Pallas kernels: none -> 3.51 us  [on_device(): pl.pallas_call(functools.partial(adjoint_kernel, sub_count, width), grid=...]
    unnamed x4 -> x6, local copies, waits for them, and re-layouts: 2.87 us -> 2.19 us
where the time goes in v2:
time: 33.9 us; the launch traced here: 33.7 us
  Pallas kernels  30.9 us (91%)
  local copies, waits for them, and re-layouts  2.19 us (6%)
  between operations  0.65 us (2%)
    pallas_call x1, Pallas kernels, on_device(): pl.pallas_call(functools.partial(kernel, facet_count, sub_count), out_sha...  27.4 us
    pallas_call x1, Pallas kernels, on_device(): pl.pallas_call(functools.partial(adjoint_kernel, sub_count, width), grid=...  3.51 us
    unnamed x6, local copies, waits for them, and re-layouts  2.19 us

profile of v2, /device:TPU:0, one launch (start us, length us, event | category | flops | bytes accessed | tf_op | source)
XLA Modules:
  0.0 33.7 jit_solution(964411476290559874)
XLA Ops:
  0.6 27.4 %shard_map.77 = (f32[128,128]{1,0:T(8,128)}, f32[2,1024]{1,0:T(2,128)}) custom-call(s32[1,2]{1,0:T(1,128)} %offsets_ref.3, bf16[1,2,16,8192]{3,2,1,0:T(8,128)(2,1)} %slab_ref.1, f32[2,1024]{1,0:T(2,128)} %position_ref.1, f32[2,1024]{1,0:T(2,128)} %observed_ref.1, s32[1,1024]{1,0:T(1,128)} %bitcast.2, s32[1,32]{1,0:T(1,128)} %bitcast.3), custom_call_target="tpu_custom_call" | custom-call | tf_op jit(solution)/shard_map/pallas_call | solution.py:412
  28.0 0.0 copy-start.2
  28.0 0.6 %copy-done.2 = s32[1,2]{1,0:T(1,128)S(1)} copy-done((s32[1,2]{1,0:T(1,128)S(1)}, s32[1,2]{1,0:T(1,128)}, u32[]{:S(2)}) %copy-start.2) | copy-done | bytes 32
  28.7 0.0 copy-start
  28.7 0.8 %copy-done = f32[128,128]{1,0:T(8,128)S(1)} copy-done((f32[128,128]{1,0:T(8,128)S(1)}, f32[128,128]{1,0:T(8,128)}, u32[]{:S(2)}) %copy-start) | copy-done | bytes 65560
  29.5 0.0 copy-start.1
  29.5 0.7 %copy-done.1 = f32[2,1024]{1,0:T(2,128)S(1)} copy-done((f32[2,1024]{1,0:T(2,128)S(1)}, f32[2,1024]{1,0:T(2,128)}, u32[]{:S(2)}) %copy-start.1) | copy-done | bytes 8216
  30.2 3.5 %shard_map.78 = (f32[1,2,16,8192]{3,2,1,0:T(8,128)}, f32[2,1024]{1,0:T(2,128)}) custom-call(s32[1,2]{1,0:T(1,128)S(1)} %copy-done.2, f32[128,128]{1,0:T(8,128)S(1)} %copy-done, f32[2,1024]{1,0:T(2,128)S(1)} %copy-done.1), custom_call_target="tpu_custom_call" | custom-call | tf_op jit(solution)/shard_map/pallas_call | solution.py:458
Async XLA Ops:
  28.0 0.7 %copy-start.2 = (s32[1,2]{1,0:T(1,128)S(1)}, s32[1,2]{1,0:T(1,128)}, u32[]{:S(2)}) copy-start(s32[1,2]{1,0:T(1,128)} %offsets_ref.3) | copy-start | bytes 28
  28.7 0.8 %copy-start = (f32[128,128]{1,0:T(8,128)S(1)}, f32[128,128]{1,0:T(8,128)}, u32[]{:S(2)}) copy-start(f32[128,128]{1,0:T(8,128)} %get-tuple-element.4.image_ref) | copy-start | bytes 196612
  29.5 0.7 %copy-start.1 = (f32[2,1024]{1,0:T(2,128)S(1)}, f32[2,1024]{1,0:T(2,128)}, u32[]{:S(2)}) copy-start(f32[2,1024]{1,0:T(2,128)} %get-tuple-element.5.found_ref) | copy-start | bytes 24580

commit v3 on v2

--- a/solution.py
+++ b/solution.py
@@ -101,10 +101,13 @@
     vis_send,
     vis_recv,
     spec_send,
+    spec_stage,
     spec_recv,
     back_send,
     back_recv,
     image_send,
+    image_stage,
+    image_sum,
     image_recv,
     place_ref,
     owner_ref,
@@ -146,16 +149,18 @@
             sub = jnp.where(sub >= sub_count, sub - sub_count, sub)
             if df or ds:
                 partners.append((facet, sub))
+    beside = partners[: sub_count - 1]
+    across = partners[sub_count - 1 :: sub_count]
 
     barrier = pltpu.get_barrier_semaphore()
     for where in partners:
         pl.semaphore_signal(barrier, inc=1, device_id=where, device_id_type=MESH)
 
-    def send_all(kind, source_of, target):
-        for facet, sub in partners:
+    def send_all(kind, peers, source_of, target):
+        for facet, sub in peers:
             pltpu.make_async_remote_copy(
                 src_ref=source_of(facet, sub),
-                dst_ref=target.at[me],
+                dst_ref=target,
                 send_sem=send_sems.at[kind],
                 recv_sem=recv_sems.at[kind],
                 device_id=(facet, sub),
@@ -163,7 +168,7 @@
             ).start()
 
     def wait_all(sems, kind, target):
-        whole = target.at[pl.ds(0, devices - 1)]
+        whole = target.at[pl.ds(0, target.shape[0] - 1)]
         pltpu.make_async_copy(whole, whole, sems.at[kind]).wait()
 
     ids = subgrid_ref[...].astype(F32)
@@ -211,7 +216,7 @@
     vis_recv[me] = vis_send[me]
 
     pl.semaphore_wait(barrier, devices - 1)
-    send_all(0, lambda f, s: vis_send.at[f * sub_count + s], vis_recv)
+    send_all(0, partners, lambda f, s: vis_send.at[f * sub_count + s], vis_recv.at[me])
 
     column_tables(offsets_ref[0, 1], columns, width, matrix, step_cos, step_sin)
     steps = width // LANES
@@ -239,10 +244,18 @@
             spectrum = straight[:, part] + pltpu.roll(crossed[:, part], SUBG, 1)
             spec_send[q + k] = spectrum.astype(BF16)
 
-    spec_recv[me] = spec_send[my_sub]
-    send_all(1, lambda f, s: spec_send.at[s], spec_recv)
+    send_all(1, beside, lambda f, s: spec_send.at[s], spec_stage.at[my_sub])
+    spec_stage[my_sub] = spec_send[my_sub]
 
     wait_all(recv_sems, 0, vis_recv)
+    for j in range(slots // LANES):
+        merged = vis_recv[j * group]
+        for i in range(1, group):
+            merged = merged + vis_recv[j * group + i]
+        known[:, j * LANES : (j + 1) * LANES] = merged
+    wait_all(recv_sems, 1, spec_stage)
+    send_all(4, across, lambda f, s: spec_stage, spec_recv.at[my_facet])
+    spec_recv[my_facet] = spec_stage[...]
     table_lane = iota((total_rows, LANES), 1)
     table_block = PR_DEV * my_facet + (table_lane >= SUBG).astype(jnp.int32)
     row_tone = table_block * (N_IMG // row_blocks) + (table_lane & (SUBG - 1))
@@ -257,12 +270,6 @@
         row_wide[at, LANES:] = rs.astype(BF16)
         row_tall[:LANES, at] = rc.T.astype(BF16)
         row_tall[LANES:, at] = rs.T.astype(BF16)
-    for j in range(slots // LANES):
-        merged = vis_recv[j * group]
-        for i in range(1, group):
-            merged = merged + vis_recv[j * group + i]
-        known[:, j * LANES : (j + 1) * LANES] = merged
-
     factor = SUBG ** (-0.5)
 
     @pl.loop(0, slots // CHUNK)
@@ -278,7 +285,7 @@
         basis_one[:, at] = jnp.concatenate([rr, -ri], 0).astype(BF16)
         basis_two[:, at] = jnp.concatenate([ri, rr], 0).astype(BF16)
 
-    wait_all(recv_sems, 1, spec_recv)
+    wait_all(recv_sems, 4, spec_recv)
     spectra = spec_recv[...].reshape(facet_count * total_rows, LANES)
     both = dot(row_tall[...], spectra)
     half = iota((1, LANES), 1) < SUBG
@@ -308,10 +315,9 @@
         weight = live * threshold / jnp.maximum(magnitude, threshold)
         wr = weight * misfit_real
         wi = weight * misfit_imag
-        blank = jnp.zeros((6, LANES), F32)
         for k in range(copies):
             part = slice(k * LANES, (k + 1) * LANES)
-            back_send[c * copies + k] = jnp.concatenate([wr[:, part], wi[:, part], blank], 0)
+            back_send[c * copies + k] = jnp.concatenate([wr[:, part], wi[:, part]], 0)
         pr = lr * wr + li * wi
         pi = lr * wi - li * wr
         pr = jnp.concatenate([jnp.where(second, 0.0, pr), jnp.where(second, pr, 0.0)], 0)
@@ -323,32 +329,41 @@
     turned = jnp.where(half, turned, -turned)
     gridded = jnp.concatenate([gridded, turned], 0).astype(BF16)
     parts = dot(row_wide[...], gridded)
-    image_send[...] = parts.astype(BF16).reshape(devices, rows, LANES)
-    send_all(3, lambda f, s: image_send.at[f * sub_count + s], image_recv)
-    send_all(2, lambda f, s: back_send.at[lax.div(f * sub_count + s, group)], back_recv)
-    image_recv[me] = image_send[me]
+    image_send[...] = parts.astype(BF16).reshape(facet_count, sub_count, rows, LANES)
+    send_all(3, across, lambda f, s: image_send.at[f], image_stage.at[my_facet])
+    send_all(
+        2, partners, lambda f, s: back_send.at[lax.div(f * sub_count + s, group)], back_recv.at[me]
+    )
+    image_stage[my_facet] = image_send[my_facet]
     back_recv[me] = back_send[lax.div(me, group)]
 
+    wait_all(recv_sems, 3, image_stage)
+    images = image_stage[0].astype(F32)
+    for f in range(1, facet_count):
+        images = images + image_stage[f].astype(F32)
+    image_sum[...] = images.astype(BF16)
+    send_all(5, beside, lambda f, s: image_sum.at[s], image_recv.at[my_sub])
+    image_recv[my_sub] = image_sum[my_sub]
+
     wait_all(recv_sems, 2, back_recv)
-    returned = back_recv[...].reshape(devices * 8, LANES)
-    found = jnp.zeros((devices * 8, vis), F32)
+    returned = back_recv[...].reshape(devices * 2, LANES)
+    found = jnp.zeros((devices * 2, vis), F32)
     for part in three_parts(returned):
         found = found + dot(part, place_ref[...])
-    chosen = iota((devices, 8, vis), 0).astype(F32) == owner_ref[...][None]
-    found = jnp.sum(jnp.where(chosen, found.reshape(devices, 8, vis), 0.0), 0)
-    residual_ref[...] = found[0:2]
-
-    wait_all(recv_sems, 3, image_recv)
-    held = image_recv[...].astype(F32).reshape(facet_count, columns * rows, LANES)
-    images = held[0]
-    for f in range(1, facet_count):
-        images = images + held[f]
-    image_ref[...] = images
+    row = iota((devices * 2, vis), 0).astype(F32)
+    wanted = owner_ref[...] * 2.0
+    residual_ref[0:1, :] = jnp.sum(jnp.where(row == wanted, found, 0.0), 0, keepdims=True)
+    residual_ref[1:2, :] = jnp.sum(jnp.where(row == wanted + 1.0, found, 0.0), 0, keepdims=True)
+
+    wait_all(recv_sems, 5, image_recv)
+    image_ref[...] = image_recv[...].astype(F32).reshape(columns * rows, LANES)
 
     wait_all(send_sems, 0, vis_recv)
-    wait_all(send_sems, 1, spec_recv)
+    wait_all(send_sems, 1, spec_stage)
     wait_all(send_sems, 2, back_recv)
-    wait_all(send_sems, 3, image_recv)
+    wait_all(send_sems, 3, image_stage)
+    wait_all(send_sems, 4, spec_recv)
+    wait_all(send_sems, 5, image_recv)
 
 
 def adjoint_kernel(
@@ -421,11 +436,14 @@
             pltpu.VMEM((devices, 8, LANES), F32),
             pltpu.VMEM((devices, 8, LANES), F32),
             pltpu.VMEM((sub_count, rows, LANES), BF16),
-            pltpu.VMEM((devices, rows, LANES), BF16),
-            pltpu.VMEM((slots // LANES, 8, LANES), F32),
-            pltpu.VMEM((devices, 8, LANES), F32),
-            pltpu.VMEM((devices, rows, LANES), BF16),
-            pltpu.VMEM((devices, rows, LANES), BF16),
+            pltpu.VMEM((sub_count, rows, LANES), BF16),
+            pltpu.VMEM((facet_count, sub_count, rows, LANES), BF16),
+            pltpu.VMEM((slots // LANES, 2, LANES), F32),
+            pltpu.VMEM((devices, 2, LANES), F32),
+            pltpu.VMEM((facet_count, sub_count, rows, LANES), BF16),
+            pltpu.VMEM((facet_count, sub_count, rows, LANES), BF16),
+            pltpu.VMEM((sub_count, rows, LANES), BF16),
+            pltpu.VMEM((sub_count, rows, LANES), BF16),
             pltpu.VMEM((LANES, vis), BF16),
             pltpu.VMEM((1, vis), F32),
             pltpu.VMEM((width // LANES * rows, 2 * LANES), BF16),
@@ -439,8 +457,8 @@
             pltpu.VMEM((2 * SUBG, slots), BF16),
             pltpu.VMEM((2 * SUBG, slots), BF16),
             pltpu.VMEM((8, slots), F32),
-            pltpu.SemaphoreType.DMA((4,)),
-            pltpu.SemaphoreType.DMA((4,)),
+            pltpu.SemaphoreType.DMA((6,)),
+            pltpu.SemaphoreType.DMA((6,)),
         ],
         compiler_params=pltpu.CompilerParams(
             collective_id=0, has_side_effects=True, vmem_limit_bytes=56 * 1024 * 1024
@@ -474,7 +492,7 @@
             pltpu.VMEM((rows, sub_count * LANES), F32),
             pltpu.VMEM((rows, sub_count * LANES), F32),
         ],
-        compiler_params=pltpu.CompilerParams(vmem_limit_bytes=32 * 1024 * 1024),
+        compiler_params=pltpu.CompilerParams(vmem_limit_bytes=60 * 1024 * 1024),
     )(facet_offsets, images, found)
 
 

time: 33.9 us -> 31.5 us (0.929)
  local copies, waits for them, and re-layouts: 2.19 us -> 0 us
    unnamed x6 -> x0, local copies, waits for them, and re-layouts: 2.19 us -> none
    pallas_call x1, Pallas kernels: 27.4 us -> 26.8 us  [on_device(): pl.pallas_call(functools.partial(kernel, facet_count, sub_count), out_sha...]
    pallas_call x1, Pallas kernels: 3.51 us -> 3.85 us  [on_device(): pl.pallas_call(functools.partial(adjoint_kernel, sub_count, width), grid=...]
where the time goes in v3:
time: 31.5 us; the launch traced here: 31.3 us
  Pallas kernels  30.6 us (97%)
  between operations  0.64 us (2%)
    pallas_call x1, Pallas kernels, on_device(): pl.pallas_call(functools.partial(kernel, facet_count, sub_count), out_sha...  26.8 us
    pallas_call x1, Pallas kernels, on_device(): pl.pallas_call(functools.partial(adjoint_kernel, sub_count, width), grid=...  3.85 us

profile of v3, /device:TPU:0, one launch (start us, length us, event | category | flops | bytes accessed | tf_op | source)
XLA Modules:
  0.0 31.3 jit_solution(13474745972809636079)
XLA Ops:
  0.6 26.8 %shard_map.77 = (f32[128,128]{1,0:T(8,128)}, f32[2,1024]{1,0:T(2,128)}) custom-call(s32[1,2]{1,0:T(1,128)} %offsets_ref.3, bf16[1,2,16,8192]{3,2,1,0:T(8,128)(2,1)} %slab_ref.1, f32[2,1024]{1,0:T(2,128)} %position_ref.1, f32[2,1024]{1,0:T(2,128)} %observed_ref.1, s32[1,1024]{1,0:T(1,128)} %bitcast.2, s32[1,32]{1,0:T(1,128)} %bitcast.3), custom_call_target="tpu_custom_call" | custom-call | tf_op jit(solution)/shard_map/pallas_call | solution.py:427
  27.4 3.9 %shard_map.78 = (f32[1,2,16,8192]{3,2,1,0:T(8,128)}, f32[2,1024]{1,0:T(2,128)}) custom-call(s32[1,2]{1,0:T(1,128)} %offsets_ref.3, f32[128,128]{1,0:T(8,128)} %get-tuple-element.4.image_ref, f32[2,1024]{1,0:T(2,128)} %get-tuple-element.5.found_ref), custom_call_target="tpu_custom_call" | custom-call | tf_op jit(solution)/shard_map/pallas_call | solution.py:476

commit v4 on v3

--- a/solution.py
+++ b/solution.py
@@ -40,6 +40,18 @@
     return cos_sin((index & (N_IMG - 1)).astype(F32) * (-1.0 / N_IMG))
 
 
+def spread_rows(first, second):
+    c1, s1 = first
+    c2, s2 = second
+    cos, sin = [], []
+    for k in range(c2.shape[0]):
+        ck = c2[k : k + 1]
+        sk = s2[k : k + 1]
+        cos.append(c1 * ck - s1 * sk)
+        sin.append(c1 * sk + s1 * ck)
+    return jnp.concatenate(cos, 0), jnp.concatenate(sin, 0)
+
+
 def iota(shape, dim):
     return lax.broadcasted_iota(jnp.int32, shape, dim)
 
@@ -67,7 +79,10 @@
 def column_tables(col_offset, columns, width, matrix_ref, step_cos, step_sin):
     lane = iota((LANES, LANES), 1)
     first_half = lane < SUBG
-    base_cos, base_sin = table((col_offset + iota((LANES, LANES), 0)) * (lane & (SUBG - 1)))
+    near = (col_offset + iota((8, LANES), 0)) * (iota((8, LANES), 1) & (SUBG - 1))
+    blocks = (LANES // 8, LANES)
+    far = iota(blocks, 0) * 8 * (iota(blocks, 1) & (SUBG - 1))
+    base_cos, base_sin = spread_rows(table(near), table(far))
     scale = width ** (-0.5)
     base_one = jnp.where(first_half, base_cos, base_sin) * scale
     base_two = jnp.where(first_half, -base_sin, base_cos) * scale
@@ -98,6 +113,8 @@
     clip_ref,
     image_ref,
     residual_ref,
+    start_send,
+    start_recv,
     vis_send,
     vis_recv,
     spec_send,
@@ -171,6 +188,39 @@
         whole = target.at[pl.ds(0, target.shape[0] - 1)]
         pltpu.make_async_copy(whole, whole, sems.at[kind]).wait()
 
+    column_tables(offsets_ref[0, 1], columns, width, matrix, step_cos, step_sin)
+    steps = width // LANES
+    for h in range(steps):
+        part = slice(h * LANES, (h + 1) * LANES)
+        for c in range(2):
+            slab_rows[h * rows : (h + 1) * rows, c * LANES : (c + 1) * LANES] = slab_ref[
+                0, c, :, part
+            ]
+    taken = 16
+    for q in range(0, columns, 2):
+        both = matrix[:, q * LANES : (q + 2) * LANES]
+        straight = jnp.zeros((rows, 2 * LANES), F32)
+        crossed = jnp.zeros((rows, 2 * LANES), F32)
+        for h in range(0, steps, taken):
+            spread = dot(slab_rows[h * rows : (h + taken) * rows, :], both)
+            for k in range(taken):
+                piece = spread[k * rows : (k + 1) * rows]
+                sc = step_cos[h + k : h + k + 1, :]
+                ss = step_sin[h + k : h + k + 1, :]
+                straight = straight + piece * jnp.concatenate([sc, sc], 1)
+                crossed = crossed + piece * jnp.concatenate([ss, ss], 1)
+        for k in range(2):
+            part = slice(k * LANES, (k + 1) * LANES)
+            spectrum = straight[:, part] + pltpu.roll(crossed[:, part], SUBG, 1)
+            spec_send[q + k] = spectrum.astype(BF16)
+
+    start_send[...] = jnp.zeros(start_send.shape, F32) + offsets_ref[0, 0].astype(F32)
+    pl.semaphore_wait(barrier, devices - 1)
+    send_all(1, beside, lambda f, s: spec_send.at[s], spec_stage.at[my_sub])
+    spec_stage[my_sub] = spec_send[my_sub]
+    send_all(6, across, lambda f, s: start_send, start_recv.at[my_facet])
+    start_recv[my_facet] = start_send[...]
+
     ids = subgrid_ref[...].astype(F32)
     block_row = jnp.floor((ids + 0.5) * (1.0 / columns))
     block_col = ids - block_row * columns
@@ -209,43 +259,32 @@
         masked = jnp.where(chosen, part.astype(F32)[None], 0.0)
         masked = masked.reshape(devices * 8, vis).astype(BF16)
         packed = packed + dot_nt(masked, place)
-    row_offset = offsets_ref[0, 0].astype(F32)
-    packed = packed.reshape(devices, 8, LANES)
-    packed = jnp.where(iota((devices, 8, LANES), 1) == 5, row_offset, packed)
-    vis_send[...] = packed
+    vis_send[...] = packed.reshape(devices, 8, LANES)
+    send_all(0, partners, lambda f, s: vis_send.at[f * sub_count + s], vis_recv.at[me])
     vis_recv[me] = vis_send[me]
 
-    pl.semaphore_wait(barrier, devices - 1)
-    send_all(0, partners, lambda f, s: vis_send.at[f * sub_count + s], vis_recv.at[me])
-
-    column_tables(offsets_ref[0, 1], columns, width, matrix, step_cos, step_sin)
-    steps = width // LANES
-    for h in range(steps):
-        part = slice(h * LANES, (h + 1) * LANES)
-        for c in range(2):
-            slab_rows[h * rows : (h + 1) * rows, c * LANES : (c + 1) * LANES] = slab_ref[
-                0, c, :, part
-            ]
-    taken = 16
-    for q in range(0, columns, 2):
-        both = matrix[:, q * LANES : (q + 2) * LANES]
-        straight = jnp.zeros((rows, 2 * LANES), F32)
-        crossed = jnp.zeros((rows, 2 * LANES), F32)
-        for h in range(0, steps, taken):
-            spread = dot(slab_rows[h * rows : (h + taken) * rows, :], both)
-            for k in range(taken):
-                piece = spread[k * rows : (k + 1) * rows]
-                sc = step_cos[h + k : h + k + 1, :]
-                ss = step_sin[h + k : h + k + 1, :]
-                straight = straight + piece * jnp.concatenate([sc, sc], 1)
-                crossed = crossed + piece * jnp.concatenate([ss, ss], 1)
-        for k in range(2):
-            part = slice(k * LANES, (k + 1) * LANES)
-            spectrum = straight[:, part] + pltpu.roll(crossed[:, part], SUBG, 1)
-            spec_send[q + k] = spectrum.astype(BF16)
-
-    send_all(1, beside, lambda f, s: spec_send.at[s], spec_stage.at[my_sub])
-    spec_stage[my_sub] = spec_send[my_sub]
+    wait_all(recv_sems, 1, spec_stage)
+    send_all(4, across, lambda f, s: spec_stage, spec_recv.at[my_facet])
+    spec_recv[my_facet] = spec_stage[...]
+
+    def row_tone(shape):
+        at = iota(shape, 1)
+        block = PR_DEV * my_facet + (at >= SUBG).astype(jnp.int32)
+        return block * (N_IMG // row_blocks) + (at & (SUBG - 1))
+
+    row_scale = 0.5 * total_rows ** (-0.5)
+    blocks = (total_rows // 8, LANES)
+    far = table(iota(blocks, 0) * 8 * row_tone(blocks))
+    wait_all(recv_sems, 6, start_recv)
+    for f in range(facet_count):
+        start = start_recv[f].astype(jnp.int32)
+        rc, rs = table((start + iota((8, LANES), 0)) * row_tone((8, LANES)))
+        rc, rs = spread_rows((rc * row_scale, rs * row_scale), far)
+        at = slice(f * total_rows, (f + 1) * total_rows)
+        row_wide[at, :LANES] = rc.astype(BF16)
+        row_wide[at, LANES:] = rs.astype(BF16)
+        row_tall[:LANES, at] = rc.T.astype(BF16)
+        row_tall[LANES:, at] = rs.T.astype(BF16)
 
     wait_all(recv_sems, 0, vis_recv)
     for j in range(slots // LANES):
@@ -253,33 +292,19 @@
         for i in range(1, group):
             merged = merged + vis_recv[j * group + i]
         known[:, j * LANES : (j + 1) * LANES] = merged
-    wait_all(recv_sems, 1, spec_stage)
-    send_all(4, across, lambda f, s: spec_stage, spec_recv.at[my_facet])
-    spec_recv[my_facet] = spec_stage[...]
-    table_lane = iota((total_rows, LANES), 1)
-    table_block = PR_DEV * my_facet + (table_lane >= SUBG).astype(jnp.int32)
-    row_tone = table_block * (N_IMG // row_blocks) + (table_lane & (SUBG - 1))
-    row_scale = 0.5 * total_rows ** (-0.5)
-    for f in range(facet_count):
-        start = vis_recv[f * sub_count][5:6, :].astype(jnp.int32)
-        rc, rs = table((start + iota((total_rows, LANES), 0)) * row_tone)
-        rc = rc * row_scale
-        rs = rs * row_scale
-        at = slice(f * total_rows, (f + 1) * total_rows)
-        row_wide[at, :LANES] = rc.astype(BF16)
-        row_wide[at, LANES:] = rs.astype(BF16)
-        row_tall[:LANES, at] = rc.T.astype(BF16)
-        row_tall[LANES:, at] = rs.T.astype(BF16)
+
     factor = SUBG ** (-0.5)
 
-    @pl.loop(0, slots // CHUNK)
-    def bases(c):
-        at = pl.ds(pl.multiple_of(c * CHUNK, CHUNK), CHUNK)
-        grid = iota((SUBG, CHUNK), 0).astype(F32) * (1.0 / SUBG)
-        lr, li = cos_sin(known[0:1, at] * grid)
+    for c in range(slots // CHUNK):
+        at = slice(c * CHUNK, (c + 1) * CHUNK)
+        near = iota((8, CHUNK), 0).astype(F32) * (1.0 / SUBG)
+        far = iota((SUBG // 8, CHUNK), 0).astype(F32) * (8.0 / SUBG)
+        u = known[0:1, at]
+        w = known[1:2, at]
+        lr, li = spread_rows(cos_sin(u * near), cos_sin(u * far))
         left_real[:, at] = lr * factor
         left_imag[:, at] = li * factor
-        rr, ri = cos_sin(known[1:2, at] * grid)
+        rr, ri = spread_rows(cos_sin(w * near), cos_sin(w * far))
         rr = rr * factor
         ri = ri * factor
         basis_one[:, at] = jnp.concatenate([rr, -ri], 0).astype(BF16)
@@ -364,6 +389,7 @@
     wait_all(send_sems, 3, image_stage)
     wait_all(send_sems, 4, spec_recv)
     wait_all(send_sems, 5, image_recv)
+    wait_all(send_sems, 6, start_recv)
 
 
 def adjoint_kernel(
@@ -433,6 +459,8 @@
         in_specs=[smem] + [vmem] * 5,
         out_specs=(vmem, vmem),
         scratch_shapes=[
+            pltpu.VMEM((8, LANES), F32),
+            pltpu.VMEM((facet_count, 8, LANES), F32),
             pltpu.VMEM((devices, 8, LANES), F32),
             pltpu.VMEM((devices, 8, LANES), F32),
             pltpu.VMEM((sub_count, rows, LANES), BF16),
@@ -457,8 +485,8 @@
             pltpu.VMEM((2 * SUBG, slots), BF16),
             pltpu.VMEM((2 * SUBG, slots), BF16),
             pltpu.VMEM((8, slots), F32),
-            pltpu.SemaphoreType.DMA((6,)),
-            pltpu.SemaphoreType.DMA((6,)),
+            pltpu.SemaphoreType.DMA((7,)),
+            pltpu.SemaphoreType.DMA((7,)),
         ],
         compiler_params=pltpu.CompilerParams(
             collective_id=0, has_side_effects=True, vmem_limit_bytes=56 * 1024 * 1024

time: 31.5 us -> 30.8 us (0.978)
  Pallas kernels: 30.6 us -> 30 us
    pallas_call x1, Pallas kernels: 26.8 us -> 26.2 us  [on_device(): pl.pallas_call(functools.partial(kernel, facet_count, sub_count), out_sha...]
where the time goes in v4:
time: 30.8 us; the launch traced here: 30.6 us
  Pallas kernels  30 us (97%)
  between operations  0.64 us (2%)
    pallas_call x1, Pallas kernels, on_device(): pl.pallas_call(functools.partial(kernel, facet_count, sub_count), out_sha...  26.2 us
    pallas_call x1, Pallas kernels, on_device(): pl.pallas_call(functools.partial(adjoint_kernel, sub_count, width), grid=...  3.78 us

profile of v4, /device:TPU:0, one launch (start us, length us, event | category | flops | bytes accessed | tf_op | source)
XLA Modules:
  0.0 30.6 jit_solution(10912621151291226930)
XLA Ops:
  0.6 26.2 %shard_map.77 = (f32[128,128]{1,0:T(8,128)}, f32[2,1024]{1,0:T(2,128)}) custom-call(s32[1,2]{1,0:T(1,128)} %offsets_ref.3, bf16[1,2,16,8192]{3,2,1,0:T(8,128)(2,1)} %slab_ref.1, f32[2,1024]{1,0:T(2,128)} %position_ref.1, f32[2,1024]{1,0:T(2,128)} %observed_ref.1, s32[1,1024]{1,0:T(1,128)} %bitcast.2, s32[1,32]{1,0:T(1,128)} %bitcast.3), custom_call_target="tpu_custom_call" | custom-call | tf_op jit(solution)/shard_map/pallas_call | solution.py:453
  26.9 3.8 %shard_map.78 = (f32[1,2,16,8192]{3,2,1,0:T(8,128)}, f32[2,1024]{1,0:T(2,128)}) custom-call(s32[1,2]{1,0:T(1,128)} %offsets_ref.3, f32[128,128]{1,0:T(8,128)} %get-tuple-element.4.image_ref, f32[2,1024]{1,0:T(2,128)} %get-tuple-element.5.found_ref), custom_call_target="tpu_custom_call" | custom-call | tf_op jit(solution)/shard_map/pallas_call | solution.py:504

commit v5 on v4

--- a/solution.py
+++ b/solution.py
@@ -250,16 +250,23 @@
     in_block = (block_at >= block_start) & (block_at < block_start + VIS_BLOCK)
     spread_out = jnp.where(in_block, 1.0, 0.0).astype(BF16)
     levels = dot(clip.astype(BF16), spread_out)[0:1] * 0.25
+    high, middle, low = three_parts(jnp.concatenate([position_ref[...], observed_ref[...]], 0))
     values = jnp.concatenate(
-        [position_ref[...], observed_ref[...], levels, jnp.zeros((3, vis), F32)], 0
+        [
+            high.astype(F32),
+            levels,
+            jnp.zeros((3, vis), F32),
+            middle.astype(F32),
+            low.astype(F32),
+        ],
+        0,
     )
-    chosen = iota((devices, 8, vis), 0).astype(F32) == owner[None]
-    packed = jnp.zeros((devices * 8, LANES), F32)
-    for part in three_parts(values):
-        masked = jnp.where(chosen, part.astype(F32)[None], 0.0)
-        masked = masked.reshape(devices * 8, vis).astype(BF16)
-        packed = packed + dot_nt(masked, place)
-    vis_send[...] = packed.reshape(devices, 8, LANES)
+    chosen = iota((devices, 16, vis), 0).astype(F32) == owner[None]
+    masked = jnp.where(chosen, values[None], 0.0).reshape(devices * 16, vis).astype(BF16)
+    packed = dot_nt(masked, place).reshape(devices, 16, LANES)
+    finer = packed[:, 8:12] + packed[:, 12:16]
+    finer = jnp.concatenate([finer, jnp.zeros((devices, 4, LANES), F32)], 1)
+    vis_send[...] = packed[:, 0:8] + finer
     send_all(0, partners, lambda f, s: vis_send.at[f * sub_count + s], vis_recv.at[me])
     vis_recv[me] = vis_send[me]
 
@@ -372,9 +379,9 @@
 
     wait_all(recv_sems, 2, back_recv)
     returned = back_recv[...].reshape(devices * 2, LANES)
-    found = jnp.zeros((devices * 2, vis), F32)
-    for part in three_parts(returned):
-        found = found + dot(part, place_ref[...])
+    parts = dot(jnp.concatenate(three_parts(returned), 0), place_ref[...])
+    count = devices * 2
+    found = parts[:count] + parts[count : 2 * count] + parts[2 * count :]
     row = iota((devices * 2, vis), 0).astype(F32)
     wanted = owner_ref[...] * 2.0
     residual_ref[0:1, :] = jnp.sum(jnp.where(row == wanted, found, 0.0), 0, keepdims=True)
@@ -405,16 +412,23 @@
     step_sin,
     straight,
     crossed,
+    image_held,
+    sems,
 ):
     rows = adjoint_ref.shape[2]
     block_steps = adjoint_ref.shape[3] // LANES
 
     @pl.when(pl.program_id(0) == 0)
     def first():
-        residual_ref[...] = found_ref[...]
+        image_copy = pltpu.make_async_copy(image_ref, image_held, sems.at[0])
+        found_copy = pltpu.make_async_copy(found_ref, residual_ref, sems.at[1])
+        image_copy.start()
+        found_copy.start()
         column_tables(offsets_ref[0, 1], columns, width, matrix, step_cos, step_sin)
+        image_copy.wait()
+        found_copy.wait()
         for q in range(columns):
-            image = image_ref[q * rows : (q + 1) * rows, :]
+            image = image_held[q * rows : (q + 1) * rows, :]
             at = slice(q * LANES, (q + 1) * LANES)
             straight[:, at] = image
             crossed[:, at] = pltpu.roll(image, SUBG, 1)
@@ -508,7 +522,7 @@
             jax.ShapeDtypeStruct(facet_slab.shape, F32),
             jax.ShapeDtypeStruct((2, vis), F32),
         ),
-        in_specs=[smem, whole(sub_count * rows, LANES), whole(2, vis)],
+        in_specs=[smem] + [pl.BlockSpec(memory_space=pl.ANY)] * 2,
         out_specs=(
             pl.BlockSpec((1, 2, rows, width // blocks), lambda i: (0, 0, 0, i)),
             whole(2, vis),
@@ -519,6 +533,8 @@
             pltpu.VMEM((width // LANES, LANES), F32),
             pltpu.VMEM((rows, sub_count * LANES), F32),
             pltpu.VMEM((rows, sub_count * LANES), F32),
+            pltpu.VMEM((sub_count * rows, LANES), F32),
+            pltpu.SemaphoreType.DMA((2,)),
         ],
         compiler_params=pltpu.CompilerParams(vmem_limit_bytes=60 * 1024 * 1024),
     )(facet_offsets, images, found)

time: 30.8 us -> 30.2 us (0.981)
  Pallas kernels: 30 us -> 29.4 us
    pallas_call x1, Pallas kernels: 26.2 us -> 25.3 us  [on_device(): pl.pallas_call(functools.partial(kernel, facet_count, sub_count), out_sha...]
    pallas_call x1, Pallas kernels: 3.78 us -> 4.11 us  [on_device(): pl.pallas_call(functools.partial(adjoint_kernel, sub_count, width), grid=...]
where the time goes in v5:
time: 30.2 us; the launch traced here: 30 us
  Pallas kernels  29.4 us (97%)
  between operations  0.64 us (2%)
    pallas_call x1, Pallas kernels, on_device(): pl.pallas_call(functools.partial(kernel, facet_count, sub_count), out_sha...  25.3 us
    pallas_call x1, Pallas kernels, on_device(): pl.pallas_call(functools.partial(adjoint_kernel, sub_count, width), grid=...  4.11 us

profile of v5, /device:TPU:0, one launch (start us, length us, event | category | flops | bytes accessed | tf_op | source)
XLA Modules:
  0.0 30.0 jit_solution(1194722774889245538)
XLA Ops:
  0.6 25.3 %shard_map.77 = (f32[128,128]{1,0:T(8,128)}, f32[2,1024]{1,0:T(2,128)}) custom-call(s32[1,2]{1,0:T(1,128)} %offsets_ref.3, bf16[1,2,16,8192]{3,2,1,0:T(8,128)(2,1)} %slab_ref.1, f32[2,1024]{1,0:T(2,128)} %position_ref.1, f32[2,1024]{1,0:T(2,128)} %observed_ref.1, s32[1,1024]{1,0:T(1,128)} %bitcast.2, s32[1,32]{1,0:T(1,128)} %bitcast.3), custom_call_target="tpu_custom_call" | custom-call | tf_op jit(solution)/shard_map/pallas_call | solution.py:467
  25.9 4.1 %shard_map.78 = (f32[1,2,16,8192]{3,2,1,0:T(8,128)}, f32[2,1024]{1,0:T(2,128)}) custom-call(s32[1,2]{1,0:T(1,128)} %offsets_ref.3, f32[128,128]{1,0:T(8,128)} %get-tuple-element.4.image_ref, f32[2,1024]{1,0:T(2,128)} %get-tuple-element.5.found_ref), custom_call_target="tpu_custom_call" | custom-call | tf_op jit(solution)/shard_map/pallas_call | solution.py:518
